TPU v7x, 32 devices: a whole 2x2x4 slice. The times are simulated.
32 devices in a mesh: design: 2 (over y), brick: 4 (over z), case: 2 (over x), sub: 2 (over core).
Axes of the slice: x: 2, y: 2, z: 4, core: 2. Of those that a mesh axis runs over, the one named last changes fastest.
Arguments:
- densities: float32 [64, 16, 128], P(('design', 'brick'), 'sub'), parts along dimension 0, may hold values from 0.1 to 1
- fixed_mask: int32 [3, 64, 16, 128], P(None, ('design', 'brick'), 'sub'), parts along dimension 1, may hold values 0 or 1
- start_field: float32 [8, 3, 64, 16, 128], P('case', None, ('design', 'brick'), 'sub'), parts along dimension 2, may hold values from -2.4 to 2.4
- load_nodes: int32 [8, 64], P('case'), may hold values from 0 to 65535
- load_forces: int32 [8, 64, 3], P('case'), may hold values from -4 to 4
- case_weights: int32 [8], replicated, may hold values from 1 to 4
- stiffness: float32 [24, 24], replicated, may hold values from -0.05 to 2, as said below
Outputs:
- displacement: float32 [8, 3, 64, 16, 128], P('case', None, ('design', 'brick'), 'sub'), parts along dimension 2
- sensitivity: float32 [64, 16, 128], P(('design', 'brick'), 'sub', 'case'), parts along dimension 0
There are 2 independent parts, one for each index of `design`. A program takes and returns all parts, laid end to end along the dimension named above; an argument that names none is the same for every part. Nothing has to cross between parts.
Inputs may be any that keep to these rules, and one draw needn't show every extreme that they name: `stiffness`: symmetric; each diagonal entry exceeds the sum of magnitudes of the other entries of its row.
All inputs are finite; a program needn't handle non-finite values. No bound on the sum of `fixed_mask` on one device may be relied on, other than what follows from the above.
Results may differ from a plain program's by a relative error of at most 0.00023.
Values sent between devices are 32-bit elements; how exact they have to be, the bound alone decides.
A program may use at most 128 MiB of HBM per device.

v0:
```python
import jax
import jax.numpy as jnp
from jax import lax
from jax.sharding import PartitionSpec as P

ITERS = 2


PENALTY = 3.0
SOFT_FLOOR = 0.001
CORNERS = [(a, b, c) for a in (0, 1) for b in (0, 1) for c in (0, 1)]


def shifted(block, axis, distance):
    devices = range(lax.axis_size(axis))
    route = [(i - distance, i) for i in devices if i - distance in devices]
    return lax.ppermute(block, axis, route)


def padded_2(cells, sides, width):
    for axis, dim in sides:
        count = lax.axis_size(axis)
        ends = count - 1
        head = lax.slice_in_dim(cells, 0, width, axis=dim)
        tail = lax.slice_in_dim(cells, cells.shape[dim] - width, cells.shape[dim], axis=dim)
        cells = jnp.concatenate(
            [
                lax.ppermute(tail, axis, [(i, (i + 1) % count) for i in range(ends)]),
                cells,
                lax.ppermute(head, axis, [((i + 1) % count, i) for i in range(ends)]),
            ],
            axis=dim,
        )
    return cells


def element_terms(window, stiffness):
    cells_x = window.shape[2] - 1
    cells_y = window.shape[3] - 1
    cells_z = window.shape[4]
    padded = jnp.pad(window, ((0, 0), (0, 0), (0, 0), (0, 0), (0, 1)))
    views = [padded[:, :, a : a + cells_x, b : b + cells_y, c : c + cells_z] for a, b, c in CORNERS]
    unscaled = None
    for k in range(8):
        term = jnp.einsum(
            "ij,cjxyz->cixyz",
            stiffness[:, 3 * k : 3 * k + 3],
            views[k],
            precision=lax.Precision.HIGHEST,
        )
        unscaled = term if unscaled is None else unscaled + term
    return (views, unscaled)


def element_energy(views, unscaled):
    total = None
    for k in range(8):
        term = jnp.sum(views[k] * unscaled[:, 3 * k : 3 * k + 3], axis=1)
        total = term if total is None else total + term
    return total


def assemble(forces, cells_z):
    summed = jnp.zeros(
        (forces.shape[0], 3, forces.shape[2] + 1, forces.shape[3] + 1, cells_z), jnp.float32
    )
    for k, (a, b, c) in enumerate(CORNERS):
        corner_part = forces[:, 3 * k : 3 * k + 3]
        corner_part = jnp.pad(corner_part, ((0, 0), (0, 0), (a, 1 - a), (b, 1 - b), (c, 0)))[
            ..., :cells_z
        ]
        summed = summed + corner_part
    return summed


def square_sums(residual):
    return lax.psum(jnp.sum(residual * residual, axis=(1, 2, 3, 4)), ("brick", "sub"))


def inner_sums(direction, image):
    return lax.psum(jnp.sum(direction * image, axis=(1, 2, 3, 4)), ("brick", "sub"))


def per_device(
    densities, fixed_mask, start_field, load_nodes, load_forces, case_weights, stiffness
):
    case_count, _, cells_x, cells_y, cells_z = start_field.shape
    free_mask = (1 - fixed_mask).astype(jnp.float32)
    element_scale = SOFT_FLOOR + (1.0 - SOFT_FLOOR) * densities**PENALTY
    total_y = cells_y * lax.axis_size("sub")
    brick_index = lax.axis_index("brick")
    sub_index = lax.axis_index("sub")
    global_x = load_nodes // (total_y * cells_z)
    global_y = load_nodes // cells_z % total_y
    global_z = load_nodes % cells_z
    local_x = global_x - brick_index * cells_x
    local_y = global_y - sub_index * cells_y
    inside = (local_x >= 0) & (local_x < cells_x) & (local_y >= 0) & (local_y < cells_y)
    local_index = jnp.where(
        inside, (local_x * cells_y + local_y) * cells_z + global_z, cells_x * cells_y * cells_z
    )

    def place_loads(targets, forces):
        blank = jnp.zeros((3, cells_x * cells_y * cells_z), jnp.float32)
        return blank.at[:, targets].add(forces.T.astype(jnp.float32), mode="drop")

    right_side = jax.vmap(place_loads)(local_index, load_forces)
    right_side = right_side.reshape(case_count, 3, cells_x, cells_y, cells_z) * free_mask
    below_x = shifted(element_scale[-1:], "brick", 1)
    scale_rows = jnp.concatenate([below_x, element_scale], axis=0)
    below_y = shifted(scale_rows[:, -1:], "sub", 1)
    scale_wide = jnp.concatenate([below_y, scale_rows], axis=1)

    def element_pass(field):
        window = padded_2(field, (("brick", 2), ("sub", 3)), 1)
        views, unscaled = element_terms(window, stiffness)
        node_forces = assemble(unscaled * scale_wide, cells_z)[
            :, :, 1 : cells_x + 1, 1 : cells_y + 1
        ]
        energy = element_energy(views, unscaled)[:, 1:, 1:]
        return (node_forces, energy)

    displace = start_field * free_mask
    residual = right_side - element_pass(displace)[0] * free_mask
    direction = residual
    norm_now = square_sums(residual)
    for iteration in range(ITERS):
        image = element_pass(direction)[0] * free_mask
        step_length = (norm_now / inner_sums(direction, image))[:, None, None, None, None]
        displace = displace + step_length * direction
        residual = residual - step_length * image
        norm_next = square_sums(residual)
        direction = residual + (norm_next / norm_now)[:, None, None, None, None] * direction
        norm_now = norm_next
    energy = element_pass(displace)[1]
    weights = case_weights.astype(jnp.float32)
    local_weights = lax.dynamic_slice_in_dim(
        weights, lax.axis_index("case") * case_count, case_count
    )
    weighted = jnp.sum(local_weights[:, None, None, None] * energy, axis=0)
    share_depth = cells_z // lax.axis_size("case")
    share_start = lax.axis_index("case") * share_depth
    summed = lax.psum(weighted, "case")
    owned_energy = lax.dynamic_slice_in_dim(summed, share_start, share_depth, 2)
    owned_density = lax.dynamic_slice_in_dim(densities, share_start, share_depth, 2)
    sensitivity = (
        -(PENALTY * (1.0 - SOFT_FLOOR))
        * owned_density ** (PENALTY - 1.0)
        * owned_energy
        / jnp.sum(weights)
    )
    return (displace, sensitivity)


def solution(mesh):
    return jax.shard_map(
        per_device,
        mesh=mesh,
        in_specs=(
            P(("design", "brick"), "sub", None),
            P(None, ("design", "brick"), "sub", None),
            P("case", None, ("design", "brick"), "sub", None),
            P("case", None),
            P("case", None, None),
            P(),
            P(),
        ),
        out_specs=(
            P("case", None, ("design", "brick"), "sub", None),
            P(("design", "brick"), "sub", "case"),
        ),
        check_vma=False,
    )
```

profile of v0, /device:TPU:0, one launch (start us, length us, event | category | flops | bytes accessed | tf_op | source)
XLA Modules:
  0.0 334.7 jit_solution(4661059587329598517)
XLA Ops:
  2.9 4.9 %collective-permute-start = (f32[4,3,1,8,128]{4,1,3,2,0:T(4,128)S(1)}, f32[4,3,1,8,128]{4,1,3,2,0:T(4,128)S(1)}, u32[]{:S(2)}, u32[]{:S(2)}) collective-permute-start(f32[4,3,1,8,128]{4,1,3,2,0:T(4,128)S(1)} %get-tuple-element.65), channel_id=1, source_target_pairs={{0,4},{4,8},{8,12},{1,5},{5,9},{9,13},{2,6},{6,10},{10,14},{3,7},{... | collective-permute-start | bytes 147464 | tf_op jit(solution)/shard_map/ppermute | solution.py:28
  10.0 4.5 %collective-permute-start.4 = (f32[1,8,128]{2,1,0:T(8,128)S(1)}, f32[1,8,128]{2,1,0:T(8,128)S(1)}, u32[]{:S(2)}, u32[]{:S(2)}) collective-permute-start(f32[1,8,128]{2,1,0:T(8,128)S(1)} %slice.488), channel_id=1, source_target_pairs={{0,4},{4,8},{8,12},{1,5},{5,9},{9,13},{2,6},{6,10},{10,14},{3,7},{... | collective-permute-start | bytes 12296 | tf_op jit(solution)/shard_map/ppermute | solution.py:17
  16.1 6.8 %broadcast_in_dim.8 = f32[4,3,8192]{1,2,0:T(8,128)} broadcast(f32[]{:T(128)} %constant.67.clone.1), dimensions={} | broadcast | bytes 393220 | tf_op jit(solution)/shard_map/vmap()/broadcast_in_dim;vmap()/broadcast_in_dim | solution.py:105
  22.9 31.1 %scatter_fusion = f32[4,3,8192]{1,2,0:T(8,128)} fusion(f32[4,3,8192]{1,2,0:T(8,128)} %broadcast_in_dim.8, s32[256]{0:T(256)S(1)} %reshape.14, f32[256,3]{1,0:T(8,128)S(1)} %bitcast.137), kind=kCustom, calls=%fused_computation | custom fusion | flops 768 | bytes 11264 | tf_op jit(solution)/shard_map/vmap()/scatter-add | solution.py:105
  54.0 10.7 %copy.39 = f32[4,3,8,8,128]{4,1,3,2,0:T(4,128)} copy(f32[4,3,8,8,128]{1,4,3,2,0:T(8,128)} %bitcast.136) | data formatting | bytes 786432 | tf_op jit(solution)/shard_map/reshape | solution.py:108
  81.0 5.0 %fusion.73 = f32[4,9,9,128,24]{3,4,2,1,0:T(8,128)} fusion(f32[4,3,10,1,128]{4,1,3,2,0:T(4,128)S(1)} %collective-permute-done.3, f32[4,3,1,8,128]{4,1,3,2,0:T(4,128)S(1)} %collective-permute-done.1, f32[4,3,8,8,128]{4,1,3,2,0:T(4,128)S(1)} %copy_multiply_fusion, f32[4,3,1,8,128]{4,1,3,2,0:T(4,128)S(1)} %collective-permute-done, f32[24,24]{1,0:T(8,128)S(1)} %copy-done), kind=kOutput, calls=%fused_computation.144 | convolution fusion | flops 36246528 | bytes 4536576 | tf_op jit(solution)/shard_map/ij,cjxyz->cixyz/dot_general | solution.py:45
  86.0 4.8 %fusion.74 = f32[4,9,9,128,24]{3,4,2,1,0:T(8,128)} fusion(f32[4,3,1,8,128]{4,1,3,2,0:T(4,128)S(1)} %collective-permute-done.1, f32[4,3,8,8,128]{4,1,3,2,0:T(4,128)S(1)} %copy_multiply_fusion, f32[4,3,1,8,128]{4,1,3,2,0:T(4,128)S(1)} %collective-permute-done, f32[4,3,10,1,128]{4,1,3,2,0:T(4,128)S(1)} %collective-permute-done.2, f32[24,24]{1,0:T(8,128)S(1)} %copy-done), kind=kOutput, calls=%fused_computation.145 | convolution fusion | flops 36246528 | bytes 4536576 | tf_op jit(solution)/shard_map/ij,cjxyz->cixyz/dot_general | solution.py:45
  90.8 4.6 %fusion.75 = f32[4,9,9,128,24]{3,4,2,1,0:T(8,128)} fusion(f32[4,3,1,8,128]{4,1,3,2,0:T(4,128)S(1)} %collective-permute-done.1, f32[4,3,8,8,128]{4,1,3,2,0:T(4,128)S(1)} %copy_multiply_fusion, f32[4,3,1,8,128]{4,1,3,2,0:T(4,128)S(1)} %collective-permute-done, f32[4,3,10,1,128]{4,1,3,2,0:T(4,128)S(1)} %collective-permute-done.2, f32[24,24]{1,0:T(8,128)S(1)} %copy-done), kind=kOutput, calls=%fused_computation.146 | convolution fusion | flops 36246528 | bytes 4536576 | tf_op jit(solution)/shard_map/ij,cjxyz->cixyz/dot_general | solution.py:45
  95.5 4.8 %fusion.72 = f32[4,9,9,128,24]{3,4,2,1,0:T(8,128)} fusion(f32[4,3,10,1,128]{4,1,3,2,0:T(4,128)S(1)} %collective-permute-done.3, f32[4,3,1,8,128]{4,1,3,2,0:T(4,128)S(1)} %collective-permute-done.1, f32[4,3,8,8,128]{4,1,3,2,0:T(4,128)S(1)} %copy_multiply_fusion, f32[4,3,1,8,128]{4,1,3,2,0:T(4,128)S(1)} %collective-permute-done, f32[24,24]{1,0:T(8,128)S(1)} %copy-done), kind=kOutput, calls=%fused_computation.143 | convolution fusion | flops 36246528 | bytes 4536576 | tf_op jit(solution)/shard_map/ij,cjxyz->cixyz/dot_general | solution.py:45
  100.3 8.0 %multiply_bitcast_fusion.2 = f32[4,24,9,9,128]{4,1,3,2,0:T(8,128)S(1)} fusion(f32[4,9,9,128,24]{3,4,2,1,0:T(8,128)} %fusion.72, f32[4,9,9,128,24]{3,4,2,1,0:T(8,128)S(1)} %fusion.40, f32[4,9,9,128,24]{3,4,2,1,0:T(8,128)} %fusion.74, f32[4,9,9,128,24]{3,4,2,1,0:T(8,128)S(1)} %fusion.42, f32[4,9,9,128,24]{3,4,2,1,0:T(8,128)} %fusion.73, ...), kind=kOutput, calls=%fused_computation.3 | convolution fusion | flops 43794432 | bytes 32600064 | tf_op jit(solution)/shard_map/ij,cjxyz->cixyz/dot_general | solution.py:45
  132.7 5.3 %fusion.34 = f32[4,9,9,128,24]{3,4,2,1,0:T(8,128)} fusion(f32[4,3,10,10,129]{4,1,3,2,0:T(4,128)S(1)} %select_maximum_fusion.8, f32[24,24]{1,0:T(8,128)S(1)} %copy-done), kind=kOutput, calls=%fused_computation.78 | convolution fusion | flops 35831808 | bytes 4657152 | tf_op jit(solution)/shard_map/ij,cjxyz->cixyz/dot_general | solution.py:45
  137.9 4.6 %fusion.71 = f32[4,9,9,128,24]{3,4,2,1,0:T(8,128)} fusion(f32[4,3,1,8,128]{4,1,3,2,0:T(4,128)S(1)} %collective-permute-done.7, f32[4,3,8,8,128]{4,1,3,2,0:T(4,128)S(1)} %fusion.61, f32[4,3,1,8,128]{4,1,3,2,0:T(4,128)S(1)} %collective-permute-done.6, f32[4,3,10,1,128]{4,1,3,2,0:T(4,128)S(1)} %collective-permute-done.8, f32[24,24]{1,0:T(8,128)S(1)} %copy-done), kind=kOutput, calls=%fused_computation.142 | convolution fusion | flops 36246528 | bytes 4536576 | tf_op jit(solution)/shard_map/ij,cjxyz->cixyz/dot_general | solution.py:45
  142.6 4.8 %fusion.69 = f32[4,9,9,128,24]{3,4,2,1,0:T(8,128)} fusion(f32[4,3,10,1,128]{4,1,3,2,0:T(4,128)S(1)} %collective-permute-done.9, f32[4,3,1,8,128]{4,1,3,2,0:T(4,128)S(1)} %collective-permute-done.7, f32[4,3,8,8,128]{4,1,3,2,0:T(4,128)S(1)} %fusion.61, f32[4,3,1,8,128]{4,1,3,2,0:T(4,128)S(1)} %collective-permute-done.6, f32[24,24]{1,0:T(8,128)S(1)} %copy-done), kind=kOutput, calls=%fused_computation.140 | convolution fusion | flops 36246528 | bytes 4536576 | tf_op jit(solution)/shard_map/ij,cjxyz->cixyz/dot_general | solution.py:45
  147.4 4.8 %fusion.70 = f32[4,9,9,128,24]{3,4,2,1,0:T(8,128)} fusion(f32[4,3,1,8,128]{4,1,3,2,0:T(4,128)S(1)} %collective-permute-done.7, f32[4,3,8,8,128]{4,1,3,2,0:T(4,128)S(1)} %fusion.61, f32[4,3,1,8,128]{4,1,3,2,0:T(4,128)S(1)} %collective-permute-done.6, f32[4,3,10,1,128]{4,1,3,2,0:T(4,128)S(1)} %collective-permute-done.8, f32[24,24]{1,0:T(8,128)S(1)} %copy-done), kind=kOutput, calls=%fused_computation.141 | convolution fusion | flops 36246528 | bytes 4536576 | tf_op jit(solution)/shard_map/ij,cjxyz->cixyz/dot_general | solution.py:45
  152.2 4.8 %fusion.68 = f32[4,9,9,128,24]{3,4,2,1,0:T(8,128)} fusion(f32[4,3,10,1,128]{4,1,3,2,0:T(4,128)S(1)} %collective-permute-done.9, f32[4,3,1,8,128]{4,1,3,2,0:T(4,128)S(1)} %collective-permute-done.7, f32[4,3,8,8,128]{4,1,3,2,0:T(4,128)S(1)} %fusion.61, f32[4,3,1,8,128]{4,1,3,2,0:T(4,128)S(1)} %collective-permute-done.6, f32[24,24]{1,0:T(8,128)S(1)} %copy-done), kind=kOutput, calls=%fused_computation.139 | convolution fusion | flops 36246528 | bytes 4536576 | tf_op jit(solution)/shard_map/ij,cjxyz->cixyz/dot_general | solution.py:45
  157.0 9.5 %multiply_bitcast_fusion.1 = f32[4,24,9,9,128]{4,1,3,2,0:T(8,128)S(1)} fusion(f32[4,9,9,128,24]{3,4,2,1,0:T(8,128)} %fusion.68, f32[4,9,9,128,24]{3,4,2,1,0:T(8,128)S(1)} %fusion.30, f32[4,9,9,128,24]{3,4,2,1,0:T(8,128)} %fusion.70, f32[4,9,9,128,24]{3,4,2,1,0:T(8,128)S(1)} %fusion.32, f32[4,9,9,128,24]{3,4,2,1,0:T(8,128)} %fusion.69, ...), kind=kOutput, calls=%fused_computation.2 | convolution fusion | flops 43794432 | bytes 32600064 | tf_op jit(solution)/shard_map/ij,cjxyz->cixyz/dot_general | solution.py:45
  169.8 13.8 %all-reduce.28 = (f32[4]{0:T(128)S(1)}, f32[4]{0:T(128)S(1)}) all-reduce(f32[4]{0:T(128)S(1)} %get-tuple-element.21, f32[4]{0:T(128)S(1)} %get-tuple-element.20), channel_id=1, replica_groups=mesh['design'=2,'brick'=4,'case'=2,'sub'=2] {'brick','sub'}, use_global_device_ids=true, to_apply=%region_2.3 | all-reduce | flops 8 | bytes 64 | tf_op jit(solution)/shard_map/psum | solution.py:77
  183.9 13.6 %psum.37 = f32[4]{0:T(128)S(1)} all-reduce(f32[4]{0:T(128)S(1)} %multiply_reduce_fusion), channel_id=1, replica_groups=mesh['design'=2,'brick'=4,'case'=2,'sub'=2] {'brick','sub'}, use_global_device_ids=true, to_apply=%region_6.7 | all-reduce | flops 4 | bytes 32 | tf_op jit(solution)/shard_map/psum | solution.py:77
  217.0 5.1 %fusion.24 = f32[4,9,9,128,24]{3,4,2,1,0:T(8,128)} fusion(f32[4,3,10,10,129]{4,1,3,2,0:T(4,128)S(1)} %select_maximum_fusion.4, f32[24,24]{1,0:T(8,128)S(1)} %copy-done), kind=kOutput, calls=%fused_computation.70 | convolution fusion | flops 35831808 | bytes 4657152 | tf_op jit(solution)/shard_map/ij,cjxyz->cixyz/dot_general | solution.py:45
  222.1 4.6 %fusion.67 = f32[4,9,9,128,24]{3,4,2,1,0:T(8,128)} fusion(f32[4,3,1,8,128]{4,1,3,2,0:T(4,128)S(1)} %collective-permute-done.11, f32[4,3,8,8,128]{4,1,3,2,0:T(4,128)S(1)} %multiply_add_fusion.1, f32[4,3,1,8,128]{4,1,3,2,0:T(4,128)S(1)} %collective-permute-done.10, f32[4,3,10,1,128]{4,1,3,2,0:T(4,128)S(1)} %collective-permute-done.12, f32[24,24]{1,0:T(8,128)S(1)} %copy-done), kind=kOutput, calls=%fused_computation.138 | convolution fusion | flops 36246528 | bytes 4536576 | tf_op jit(solution)/shard_map/ij,cjxyz->cixyz/dot_general | solution.py:45
  226.8 4.8 %fusion.65 = f32[4,9,9,128,24]{3,4,2,1,0:T(8,128)} fusion(f32[4,3,10,1,128]{4,1,3,2,0:T(4,128)S(1)} %collective-permute-done.13, f32[4,3,1,8,128]{4,1,3,2,0:T(4,128)S(1)} %collective-permute-done.11, f32[4,3,8,8,128]{4,1,3,2,0:T(4,128)S(1)} %multiply_add_fusion.1, f32[4,3,1,8,128]{4,1,3,2,0:T(4,128)S(1)} %collective-permute-done.10, f32[24,24]{1,0:T(8,128)S(1)} %copy-done), kind=kOutput, calls=%fused_computation.136 | convolution fusion | flops 36246528 | bytes 4536576 | tf_op jit(solution)/shard_map/ij,cjxyz->cixyz/dot_general | solution.py:45
  231.6 4.8 %fusion.66 = f32[4,9,9,128,24]{3,4,2,1,0:T(8,128)} fusion(f32[4,3,1,8,128]{4,1,3,2,0:T(4,128)S(1)} %collective-permute-done.11, f32[4,3,8,8,128]{4,1,3,2,0:T(4,128)S(1)} %multiply_add_fusion.1, f32[4,3,1,8,128]{4,1,3,2,0:T(4,128)S(1)} %collective-permute-done.10, f32[4,3,10,1,128]{4,1,3,2,0:T(4,128)S(1)} %collective-permute-done.12, f32[24,24]{1,0:T(8,128)S(1)} %copy-done), kind=kOutput, calls=%fused_computation.137 | convolution fusion | flops 36246528 | bytes 4536576 | tf_op jit(solution)/shard_map/ij,cjxyz->cixyz/dot_general | solution.py:45
  236.3 4.8 %fusion.64 = f32[4,9,9,128,24]{3,4,2,1,0:T(8,128)} fusion(f32[4,3,10,1,128]{4,1,3,2,0:T(4,128)S(1)} %collective-permute-done.13, f32[4,3,1,8,128]{4,1,3,2,0:T(4,128)S(1)} %collective-permute-done.11, f32[4,3,8,8,128]{4,1,3,2,0:T(4,128)S(1)} %multiply_add_fusion.1, f32[4,3,1,8,128]{4,1,3,2,0:T(4,128)S(1)} %collective-permute-done.10, f32[24,24]{1,0:T(8,128)S(1)} %copy-done), kind=kOutput, calls=%fused_computation.135 | convolution fusion | flops 36246528 | bytes 4536576 | tf_op jit(solution)/shard_map/ij,cjxyz->cixyz/dot_general | solution.py:45
  241.1 9.3 %multiply_bitcast_fusion = f32[4,24,9,9,128]{4,1,3,2,0:T(8,128)S(1)} fusion(f32[4,9,9,128,24]{3,4,2,1,0:T(8,128)} %fusion.64, f32[4,9,9,128,24]{3,4,2,1,0:T(8,128)S(1)} %fusion.20, f32[4,9,9,128,24]{3,4,2,1,0:T(8,128)} %fusion.66, f32[4,9,9,128,24]{3,4,2,1,0:T(8,128)S(1)} %fusion.22, f32[4,9,9,128,24]{3,4,2,1,0:T(8,128)} %fusion.65, ...), kind=kOutput, calls=%fused_computation.1 | convolution fusion | flops 43794432 | bytes 32600064 | tf_op jit(solution)/shard_map/ij,cjxyz->cixyz/dot_general | solution.py:45
  253.7 13.7 %psum.38 = f32[4]{0:T(128)S(1)} all-reduce(f32[4]{0:T(128)S(1)} %fusion.58), channel_id=1, replica_groups=mesh['design'=2,'brick'=4,'case'=2,'sub'=2] {'brick','sub'}, use_global_device_ids=true, to_apply=%region_8.9 | all-reduce | flops 4 | bytes 32 | tf_op jit(solution)/shard_map/psum | solution.py:81
  291.4 4.8 %fusion.109 = f32[4,9,9,128,24]{3,4,2,1,0:T(8,128)} fusion(f32[24,24]{1,0:T(8,128)S(1)} %copy-done, f32[4,3,1,8,128]{4,1,3,2,0:T(4,128)S(1)} %collective-permute-done.15, f32[4,3,8,8,128]{4,1,3,2,0:T(4,128)S(1)} %multiply_add_fusion, f32[4,3,1,8,128]{4,1,3,2,0:T(4,128)S(1)} %collective-permute-done.14, f32[4,3,10,1,128]{4,1,3,2,0:T(4,128)S(1)} %collective-permute-done.16), kind=kOutput, calls=%fused_computation.196 | convolution fusion | flops 36246528 | bytes 4536576 | tf_op jit(solution)/shard_map/ij,cjxyz->cixyz/dot_general | solution.py:45
  296.2 4.8 %fusion.100 = f32[4,9,9,128,24]{3,4,2,1,0:T(8,128)} fusion(f32[24,24]{1,0:T(8,128)S(1)} %copy-done, f32[4,3,10,1,128]{4,1,3,2,0:T(4,128)S(1)} %collective-permute-done.17, f32[4,3,1,8,128]{4,1,3,2,0:T(4,128)S(1)} %collective-permute-done.15, f32[4,3,8,8,128]{4,1,3,2,0:T(4,128)S(1)} %multiply_add_fusion, f32[4,3,1,8,128]{4,1,3,2,0:T(4,128)S(1)} %collective-permute-done.14), kind=kOutput, calls=%fused_computation.187 | convolution fusion | flops 36246528 | bytes 4536576 | tf_op jit(solution)/shard_map/ij,cjxyz->cixyz/dot_general | solution.py:45
  301.0 4.8 %fusion.91 = f32[4,9,9,128,24]{3,4,2,1,0:T(8,128)} fusion(f32[24,24]{1,0:T(8,128)S(1)} %copy-done, f32[4,3,1,8,128]{4,1,3,2,0:T(4,128)S(1)} %collective-permute-done.15, f32[4,3,8,8,128]{4,1,3,2,0:T(4,128)S(1)} %multiply_add_fusion, f32[4,3,1,8,128]{4,1,3,2,0:T(4,128)S(1)} %collective-permute-done.14, f32[4,3,10,1,128]{4,1,3,2,0:T(4,128)S(1)} %collective-permute-done.16), kind=kOutput, calls=%fused_computation.178 | convolution fusion | flops 36246528 | bytes 4536576 | tf_op jit(solution)/shard_map/ij,cjxyz->cixyz/dot_general | solution.py:45
  305.8 4.8 %fusion.82 = f32[4,9,9,128,24]{3,4,2,1,0:T(8,128)} fusion(f32[24,24]{1,0:T(8,128)S(1)} %copy-done, f32[4,3,10,1,128]{4,1,3,2,0:T(4,128)S(1)} %collective-permute-done.17, f32[4,3,1,8,128]{4,1,3,2,0:T(4,128)S(1)} %collective-permute-done.15, f32[4,3,8,8,128]{4,1,3,2,0:T(4,128)S(1)} %multiply_add_fusion, f32[4,3,1,8,128]{4,1,3,2,0:T(4,128)S(1)} %collective-permute-done.14), kind=kOutput, calls=%fused_computation.169 | convolution fusion | flops 36246528 | bytes 4536576 | tf_op jit(solution)/shard_map/ij,cjxyz->cixyz/dot_general | solution.py:45
  310.6 8.5 %add_bitcast_fusion = f32[4,24,9,9,128]{4,1,3,2,0:T(8,128)S(1)} fusion(f32[4,9,9,128,24]{3,4,2,1,0:T(8,128)} %fusion.82, f32[4,9,9,128,24]{3,4,2,1,0:T(8,128)S(1)} %fusion.50, f32[4,9,9,128,24]{3,4,2,1,0:T(8,128)} %fusion.91, f32[4,9,9,128,24]{3,4,2,1,0:T(8,128)S(1)} %fusion.52, f32[4,9,9,128,24]{3,4,2,1,0:T(8,128)} %fusion.100, ...), kind=kOutput, calls=%fused_computation.4 | convolution fusion | flops 42799104 | bytes 32526336 | tf_op jit(solution)/shard_map/ij,cjxyz->cixyz/dot_general | solution.py:45
  319.4 4.8 %fusion.14 = (f32[4,9,9,128]{3,2,1,0:T(8,128)S(1)}, f32[4,9,9,128]{3,2,1,0:T(8,128)S(1)}, f32[4,9,9,128]{3,2,1,0:T(8,128)S(1)}, f32[4,9,9,128]{3,2,1,0:T(8,128)S...) fusion(f32[4,24,9,9,128]{4,1,3,2,0:T(8,128)S(1)} %add_bitcast_f, ...), kind=kLoop, calls=%fused_computation.61 | loop fusion | flops 1658880 | bytes 9289728 | tf_op jit(solution)/shard_map/reduce_sum | solution.py:58
  324.4 8.8 %psum.39 = f32[8,8,128]{2,1,0:T(8,128)S(1)} all-reduce(f32[8,8,128]{2,1,0:T(8,128)S(1)} %fusion.63), channel_id=1, replica_groups=mesh['design'=2,'brick'=4,'case'=2,'sub'=2] {'case'}, use_global_device_ids=true, to_apply=%region_18.19 | all-reduce | flops 8192 | bytes 65536 | tf_op jit(solution)/shard_map/psum | solution.py:143
  (105 shorter events, 98.3 us)
Async XLA Ops:
  2.9 63.1 %collective-permute-start = (f32[4,3,1,8,128]{4,1,3,2,0:T(4,128)S(1)}, f32[4,3,1,8,128]{4,1,3,2,0:T(4,128)S(1)}, u32[]{:S(2)}, u32[]{:S(2)}) collective-permute-start(f32[4,3,1,8,128]{4,1,3,2,0:T(4,128)S(1)} %get-tuple-element.65), channel_id=1, source_target_pairs={{0,4},{4,8},{8,12},{1,5},{5,9},{9,13},{2,6},{6,10},{10,14},{3,7},{... | collective-permute-start | bytes 147464 | tf_op jit(solution)/shard_map/ppermute | solution.py:28
  7.9 58.1 %collective-permute-start.1 = (f32[4,3,1,8,128]{4,1,3,2,0:T(4,128)S(1)}, f32[4,3,1,8,128]{4,1,3,2,0:T(4,128)S(1)}, u32[]{:S(2)}, u32[]{:S(2)}) collective-permute-start(f32[4,3,1,8,128]{4,1,3,2,0:T(4,128)S(1)} %get-tuple-element.66), channel_id=1, source_target_pairs={{4,0},{8,4},{12,8},{5,1},{9,5},{13,9},{6,2},{10,6},{14,10},{7,3},{... | collective-permute-start | bytes 147464 | tf_op jit(solution)/shard_map/ppermute | solution.py:30
  10.0 54.7 %collective-permute-start.4 = (f32[1,8,128]{2,1,0:T(8,128)S(1)}, f32[1,8,128]{2,1,0:T(8,128)S(1)}, u32[]{:S(2)}, u32[]{:S(2)}) collective-permute-start(f32[1,8,128]{2,1,0:T(8,128)S(1)} %slice.488), channel_id=1, source_target_pairs={{0,4},{4,8},{8,12},{1,5},{5,9},{9,13},{2,6},{6,10},{10,14},{3,7},{... | collective-permute-start | bytes 12296 | tf_op jit(solution)/shard_map/ppermute | solution.py:17
  54.0 16.9 %copy-start = (f32[24,24]{1,0:T(8,128)S(1)}, f32[24,24]{1,0:T(8,128)}, u32[]{:S(2)}) copy-start(f32[24,24]{1,0:T(8,128)} %param.13) | copy-start | bytes 6916
  64.7 4.4 %collective-permute-start.5 = (f32[9,1,128]{2,1,0:T(1,128)S(1)}, f32[9,1,128]{2,1,0:T(1,128)S(1)}, u32[]{:S(2)}, u32[]{:S(2)}) collective-permute-start(f32[9,1,128]{2,1,0:T(1,128)S(1)} %pad_maximum_fusion.22), channel_id=1, source_target_pairs={{0,1},{2,3},{4,5},{6,7},{8,9},{10,11},{12,13},{14,15},{16,17},{18,... | collective-permute-start | bytes 13832 | tf_op jit(solution)/shard_map/ppermute | solution.py:17
  66.1 3.1 collective-permute-start.2
  67.4 3.2 collective-permute-start.3
  109.2 1.5 copy-start.1
  111.3 5.4 %collective-permute-start.6 = (f32[4,3,1,8,128]{4,1,3,2,0:T(4,128)S(1)}, f32[4,3,1,8,128]{4,1,3,2,0:T(4,128)S(1)}, u32[]{:S(2)}, u32[]{:S(2)}) collective-permute-start(f32[4,3,1,8,128]{4,1,3,2,0:T(4,128)S(1)} %get-tuple-element.63), channel_id=1, source_target_pairs={{0,4},{4,8},{8,12},{1,5},{5,9},{9,13},{2,6},{6,10},{10,14},{3,7},{... | collective-permute-start | bytes 147464 | tf_op jit(solution)/shard_map/ppermute | solution.py:28
  114.7 6.2 %collective-permute-start.7 = (f32[4,3,1,8,128]{4,1,3,2,0:T(4,128)S(1)}, f32[4,3,1,8,128]{4,1,3,2,0:T(4,128)S(1)}, u32[]{:S(2)}, u32[]{:S(2)}) collective-permute-start(f32[4,3,1,8,128]{4,1,3,2,0:T(4,128)S(1)} %get-tuple-element.64), channel_id=1, source_target_pairs={{4,0},{8,4},{12,8},{5,1},{9,5},{13,9},{6,2},{10,6},{14,10},{7,3},{... | collective-permute-start | bytes 147464 | tf_op jit(solution)/shard_map/ppermute | solution.py:30
  120.9 2.8 collective-permute-start.8
  122.2 3.2 collective-permute-start.9
  197.8 3.2 collective-permute-start.10
  199.1 6.2 %collective-permute-start.11 = (f32[4,3,1,8,128]{4,1,3,2,0:T(4,128)S(1)}, f32[4,3,1,8,128]{4,1,3,2,0:T(4,128)S(1)}, u32[]{:S(2)}, u32[]{:S(2)}) collective-permute-start(f32[4,3,1,8,128]{4,1,3,2,0:T(4,128)S(1)} %get-tuple-element.62), channel_id=1, source_target_pairs={{4,0},{8,4},{12,8},{5,1},{9,5},{13,9},{6,2},{10,6},{14,10},{7,3},{... | collective-permute-start | bytes 147464 | tf_op jit(solution)/shard_map/ppermute | solution.py:30
  205.3 2.6 collective-permute-start.12
  206.6 3.2 collective-permute-start.13
  253.0 18.4 %copy-start.3 = (s32[8]{0:T(128)S(1)}, s32[8]{0:T(128)}, u32[]{:S(2)}) copy-start(s32[8]{0:T(128)} %param.12) | copy-start | bytes 100
  268.9 3.2 collective-permute-start.14
  270.2 6.2 %collective-permute-start.15 = (f32[4,3,1,8,128]{4,1,3,2,0:T(4,128)S(1)}, f32[4,3,1,8,128]{4,1,3,2,0:T(4,128)S(1)}, u32[]{:S(2)}, u32[]{:S(2)}) collective-permute-start(f32[4,3,1,8,128]{4,1,3,2,0:T(4,128)S(1)} %get-tuple-element.60), channel_id=1, source_target_pairs={{4,0},{8,4},{12,8},{5,1},{9,5},{13,9},{6,2},{10,6},{14,10},{7,3},{... | collective-permute-start | bytes 147464 | tf_op jit(solution)/shard_map/ppermute | solution.py:30
  276.4 4.4 %collective-permute-start.16 = (f32[4,3,10,1,128]{4,1,3,2,0:T(4,128)S(1)}, f32[4,3,10,1,128]{4,1,3,2,0:T(4,128)S(1)}, u32[]{:S(2)}, u32[]{:S(2)}) collective-permute-start(f32[4,3,10,1,128]{4,1,3,2,0:T(4,128)S(1)} %get-tuple-element.51), channel_id=1, source_target_pairs={{0,1},{2,3},{4,5},{6,7},{8,9},{10,11},{12,13},{14,15},{16,17},{18,... | collective-permute-start | bytes 184328 | tf_op jit(solution)/shard_map/ppermute | solution.py:28
  277.7 3.2 collective-permute-start.17
  319.4 13.8 %copy-start.2 = (f32[8,8,128]{2,1,0:T(8,128)S(1)}, f32[8,8,128]{2,1,0:T(8,128)}, u32[]{:S(2)}) copy-start(f32[8,8,128]{2,1,0:T(8,128)} %param.7) | copy-start | bytes 98308
where the time goes:
time: 339 us; the launch traced here: 335 us
  matrix products  156 us (46%)
  blocking collectives  49.8 us (15%)
  other arithmetic  49.7 us (15%)
  starting transfers between devices  33.4 us (10%)
  local copies, waits for them, and re-layouts  24.6 us (7%)
  waiting for transfers between devices  19.4 us (6%)
    dot_general x32, matrix products, element_terms(): jnp.einsum('ij,cjxyz->cixyz', stiffness[:, 3 * k:3 * k + 3], views[k], pr...  156 us
    scatter-add x2, other arithmetic, place_loads(): return blank.at[:, targets].add(forces.T.astype(jnp.float32), mode='drop')  31.8 us
    psum x2, blocking collectives, square_sums(): lax.psum(jnp.sum(residual * residual, axis=(1, 2, 3, 4)), ('brick', 'sub'))  27.3 us
    ppermute x8, waiting for transfers between devices, padded_2(): lax.ppermute(head, axis, [((i + 1) % count, i) for i in range(ends)])  17.8 us
    ppermute x8, starting transfers between devices, padded_2(): lax.ppermute(tail, axis, [(i, (i + 1) % count) for i in range(ends)])  16.2 us
    psum x1, blocking collectives, inner_sums(): lax.psum(jnp.sum(direction * image, axis=(1, 2, 3, 4)), ('brick', 'sub'))  13.7 us
    ppermute x8, starting transfers between devices, padded_2(): lax.ppermute(head, axis, [((i + 1) % count, i) for i in range(ends)])  11.4 us
    reshape x1, local copies, waits for them, and re-layouts, per_device(): right_side.reshape(case_count, 3, cells_x, cells_y, cells_z) * free_mask  10.7 us
  transfers between devices with their start and end apart: 18, of which 10 were waited for; matrix products, arithmetic and copies ran while one was open for 16% of the time, Pallas kernels for 0%

commit v1 on v0

v1 whole, which is shorter than its diff:
```python
import functools

import jax
import jax.numpy as jnp
import numpy as np
from jax import lax
from jax.experimental import pallas as pl
from jax.experimental.pallas import tpu as pltpu
from jax.sharding import PartitionSpec as P

PENALTY = 3.0
SOFT_FLOOR = 0.001
MESH = pl.DeviceIdType.MESH
ROWS = 8
LANES = 128


def corner_index(a, b, c, comp):
    return 3 * (4 * a + 2 * b + c) + comp


def force_constants():
    pick = np.zeros((2, 96, 24), np.float32)
    spread = np.zeros((2, 24, 224), np.float32)
    keep = np.zeros((2, 2, 96, 224), np.float32)
    rows = []
    for a in (0, 1):
        for c in (0, 1):
            for comp in range(3):
                for y in range(ROWS):
                    for b in (0, 1):
                        pick[b, len(rows), corner_index(a, b, c, comp)] = 1
                    rows.append(y)
    for side in (0, 1):
        columns = []
        for a in (0, 1):
            for b in (0, 1):
                for c in (0, 1):
                    for comp in range(3):
                        for y in range(ROWS):
                            columns.append((corner_index(a, b, c, comp), y - b))
            for c in (0, 1):
                for comp in range(ROWS):
                    if comp < 3:
                        b = 1 - side
                        columns.append((corner_index(a, b, c, comp), 7 if side == 0 else -1))
                    else:
                        columns.append(None)
        for n, column in enumerate(columns):
            if column is None:
                continue
            spread[side, column[0], n] = 1
            for m, y in enumerate(rows):
                if y - column[1] in (0, 1):
                    keep[side, y - column[1], m, n] = 1
    return pick, spread, keep


def energy_constants():
    pick = np.zeros((192, 24), np.float32)
    spread = np.zeros((2, 24, 128), np.float32)
    keep = np.zeros((2, 2, 192, 128), np.float32)
    for j in range(24):
        pick[8 * j : 8 * j + 8, j] = 1
    for side in (0, 1):
        for a in (0, 1):
            for c in (0, 1):
                for comp in range(3):
                    for b in (0, 1):
                        for y in range(ROWS):
                            n = 64 * a + 24 * c + 8 * comp + y
                            spread[b, corner_index(a, b, c, comp), n] = 1
                            if y - b >= 0:
                                keep[side, b, y - b :: 8, n] = 1
                        n = 64 * a + 48 + 8 * c + comp
                        spread[b, corner_index(a, b, c, comp), n] = 1
                        if side == 0 and b == 1:
                            keep[side, b, 7::8, n] = 1
    return pick, spread, keep


def split(value):
    high = value.astype(jnp.bfloat16)
    return high, (value - high.astype(jnp.float32)).astype(jnp.bfloat16)


def exact_dot(a, b):
    return jnp.dot(a, b, precision=lax.Precision.HIGHEST, preferred_element_type=jnp.float32)


def dot16(a, b):
    return jnp.dot(a, b, preferred_element_type=jnp.float32)


def kernel(
    sizes,
    dens_ref, mask_ref, start_ref, nodes_ref, forces_ref, weights_ref, stiff_ref,
    pick_ref, spread_ref, keep_ref, pick3_ref, spread3_ref, keep3_ref,
    disp_ref, sens_ref,
    u_f, d_f, q_f, r_f, g_f, u_h, d_h, q_h, r_h, stage,
    terms, before, loads, free, dens_own, dens_side, s_own, s_shift, s_edge,
    m_hi, m_lo, n_hi, n_lo, sums, sums_out, energy, energy_in,
    send_sem, recv_sem, dsend_sem, drecv_sem, psend_sem, precv_sem, esend_sem, erecv_sem,
):
    bricks, cases, count, nx, total_y = sizes
    lanes = count * LANES
    brick = lax.axis_index("brick")
    sub = lax.axis_index("sub")
    case = lax.axis_index("case")
    group = 2 * bricks
    me = 2 * brick + sub
    last = bricks - 1
    other = 1 - sub

    def peer(k):
        target = lax.rem(me + k, group)
        return {"brick": target // 2, "sub": lax.rem(target, 2)}

    def case_peer(k):
        return {"case": lax.rem(case + k, cases)}

    barrier = pltpu.get_barrier_semaphore()
    for k in range(1, group):
        pl.semaphore_signal(barrier, inc=1, device_id=peer(k), device_id_type=MESH)
    for k in range(1, cases):
        pl.semaphore_signal(barrier, inc=1, device_id=case_peer(k), device_id_type=MESH)

    def remote(src, dst, send, recv, device):
        return pltpu.make_async_remote_copy(
            src_ref=src, dst_ref=dst, send_sem=send, recv_sem=recv,
            device_id=device, device_id_type=MESH,
        )

    lower = {"brick": brick - 1}
    upper = {"brick": brick + 1}
    lower_side = {"brick": brick - 1, "sub": other}
    upper_side = {"brick": brick + 1, "sub": other}

    def halo_copies(k, field, rows):
        def sems(n):
            return send_sem.at[k, n], recv_sem.at[k, n]

        return (
            remote(stage.at[k], rows.at[pl.ds(1, nx)], *sems(0), {"sub": other}),
            remote(field.at[1], field.at[nx + 1], *sems(1), lower),
            remote(stage.at[k, 0], rows.at[nx + 1], *sems(2), lower_side),
            remote(field.at[nx], field.at[0], *sems(3), upper),
            remote(stage.at[k, nx - 1], rows.at[0], *sems(4), upper_side),
        )

    def send_halo(k, field, rows):
        line = 7 * (1 - sub)
        stage[k] = jnp.zeros((nx, ROWS, lanes), jnp.float32)
        for x in range(nx):
            for comp in range(3):
                stage[k, x, comp : comp + 1, :] = field[x + 1, pl.ds(8 * comp + line, 1), :]
        copies = halo_copies(k, field, rows)
        copies[0].start()

        @pl.when(brick > 0)
        def _():
            copies[1].start()
            copies[2].start()

        @pl.when(brick < last)
        def _():
            copies[3].start()
            copies[4].start()

    def wait_halo(k, field, rows):
        copies = halo_copies(k, field, rows)
        copies[0].wait()

        @pl.when(brick > 0)
        def _():
            copies[1].wait_send()
            copies[2].wait_send()
            copies[3].wait_recv()
            copies[4].wait_recv()

        @pl.when(brick < last)
        def _():
            copies[3].wait_send()
            copies[4].wait_send()
            copies[1].wait_recv()
            copies[2].wait_recv()

    def density_copies():
        return (
            remote(dens_ref, dens_side.at[pl.ds(1, nx)], dsend_sem.at[0], drecv_sem.at[0], {"sub": other}),
            remote(dens_ref.at[nx - 1], dens_own.at[0], dsend_sem.at[1], drecv_sem.at[1], upper),
            remote(dens_ref.at[nx - 1], dens_side.at[0], dsend_sem.at[2], drecv_sem.at[2], upper_side),
        )

    def sum_copies(k):
        return [
            remote(sums_out.at[k], sums.at[k, n - 1], psend_sem.at[k, n - 1], precv_sem.at[k, n - 1], peer(n))
            for n in range(1, group)
        ]

    def send_sums(k, parts):
        sums_out[k] = jnp.zeros(sums_out.shape[1:], jnp.float32)
        for q, part in enumerate(parts):
            line = jnp.sum(part, axis=0, keepdims=True)
            for c in range(count):
                row = q * count + c
                sums_out[k, row : row + 1, :] = line[:, c * LANES : (c + 1) * LANES]
        for copy in sum_copies(k):
            copy.start()

    def wait_sums(k):
        for copy in sum_copies(k):
            copy.wait()
        total = sums_out[k]
        for n in range(group - 1):
            total = total + sums[k, n]
        return jnp.sum(total, axis=1, keepdims=True)

    def widen(column):
        return jnp.concatenate(
            [jnp.broadcast_to(column[c : c + 1], (1, LANES)) for c in range(count)], axis=1
        )

    def over_cases(tile):
        return jnp.concatenate([tile] * count, axis=1)

    for x in range(nx):
        for comp in range(3):
            tile = (1 - mask_ref[comp, x]).astype(jnp.float32)
            free[x, 8 * comp : 8 * comp + 8, :] = tile
            for c in range(count):
                u_f[x + 1, 8 * comp : 8 * comp + 8, c * LANES : (c + 1) * LANES] = (
                    start_ref[c, comp, x] * tile
                )
    no_plane = jnp.zeros((24, lanes), jnp.float32)
    no_rows = jnp.zeros((ROWS, lanes), jnp.float32)
    no_tile = jnp.zeros((ROWS, LANES), jnp.float32)

    @pl.when(brick == 0)
    def _():
        for field in (u_f, d_f, q_f):
            field[0] = no_plane
        for rows in (u_h, d_h, q_h):
            rows[0] = no_rows
        dens_own[0] = no_tile
        dens_side[0] = no_tile

    @pl.when(brick == last)
    def _():
        for field in (u_f, d_f, q_f):
            field[nx + 1] = no_plane
        for rows in (u_h, d_h, q_h):
            rows[nx + 1] = no_rows

    pl.semaphore_wait(barrier, group - 1 + cases - 1)
    send_halo(0, u_f, u_h)
    copies = density_copies()
    copies[0].start()

    @pl.when(brick < last)
    def _():
        copies[1].start()
        copies[2].start()

    stiff = stiff_ref[...]
    spread_stiff = exact_dot(stiff, spread_ref[sub])
    matrix = keep_ref[sub, 0] * exact_dot(pick_ref[0], spread_stiff)
    matrix = matrix + keep_ref[sub, 1] * exact_dot(pick_ref[1], spread_stiff)
    m_hi[...], m_lo[...] = split(matrix)
    matrix = None
    for b in (0, 1):
        part = keep3_ref[sub, b] * exact_dot(pick3_ref[...], exact_dot(stiff, spread3_ref[b]))
        matrix = part if matrix is None else matrix + part
    high, low = split(matrix)
    n_hi[...] = high
    n_lo[...] = low

    y_bits = int(total_y).bit_length() - 1
    z_bits = LANES.bit_length() - 1
    load_count = nodes_ref.shape[1]
    for c in range(count):
        node = nodes_ref[c : c + 1, :]
        place_z = node & (LANES - 1)
        place_y = ((node >> z_bits) & (total_y - 1)) - sub * ROWS
        place_x = (node >> (z_bits + y_bits)) - brick * nx
        inside = (place_y >= 0) & (place_y < ROWS) & (place_x >= 0) & (place_x < nx)
        place = jnp.where(inside, place_x * ROWS + place_y, -1)
        hit = lax.broadcasted_iota(jnp.int32, (nx * ROWS, load_count), 0) == place
        depth = lax.broadcasted_iota(jnp.int32, (LANES, load_count), 0) == place_z
        depth = jnp.where(depth, 1.0, 0.0).astype(jnp.bfloat16)
        for comp in range(3):
            force = forces_ref[c, comp : comp + 1, :].astype(jnp.float32)
            weighted = jnp.where(hit, force, 0.0).astype(jnp.bfloat16)
            block = lax.dot_general(
                weighted, depth, (((1,), (1,)), ((), ())), preferred_element_type=jnp.float32
            )
            for x in range(nx):
                loads[x, 8 * comp : 8 * comp + 8, c * LANES : (c + 1) * LANES] = block[8 * x : 8 * x + 8]

    copies = density_copies()
    copies[0].wait()

    @pl.when(brick < last)
    def _():
        copies[1].wait_send()
        copies[2].wait_send()

    @pl.when(brick > 0)
    def _():
        copies[1].wait_recv()
        copies[2].wait_recv()

    row_number = lax.broadcasted_iota(jnp.int32, (ROWS, LANES), 0)
    dens_own[1 : nx + 1] = dens_ref[...]
    for i in range(nx + 1):
        def scale_of(density):
            scale = SOFT_FLOOR + (1.0 - SOFT_FLOOR) * (density * density * density)
            return jnp.where(brick > 0, scale, 0.0) if i == 0 else scale

        own = scale_of(dens_own[i])
        below = jnp.where(sub > 0, scale_of(dens_side[i]), 0.0)
        own_edge = jnp.broadcast_to(own[7:8], (ROWS, LANES))
        below_edge = jnp.broadcast_to(below[7:8], (ROWS, LANES))
        s_own[i] = own
        s_shift[i] = jnp.where(row_number == 0, below_edge, pltpu.roll(own, 1, 0))
        s_edge[i] = jnp.where(sub > 0, below_edge, own_edge)

    def by_case(value, shift, edge):
        parts = []
        for c in range(count):
            part = value[:, c * LANES : (c + 1) * LANES]
            part = pltpu.roll(part, shift, 1)
            at = lax.broadcasted_iota(jnp.int32, part.shape, 1)
            parts.append(jnp.where(at == edge, 0.0, part))
        return jnp.concatenate(parts, axis=1)

    def ahead(value):
        return by_case(value, LANES - 1, LANES - 1)

    def behind(value):
        return by_case(value, 1, 0)

    def prepare(p, field, rows):
        value = field[p]
        edge = rows[p]
        terms[p, 0:24, :] = value
        terms[p, 24:48, :] = ahead(value)
        terms[p, 48:56, :] = edge
        terms[p, 56:64, :] = ahead(edge)

    def layer_forces(i):
        own = over_cases(s_own[i])[None]
        shift = over_cases(s_shift[i])[None]
        edge = over_cases(s_edge[i])[None]
        parts = []
        for a in (0, 1):
            main = terms[i + a, 0:48, :].reshape(6, ROWS, lanes)
            side = terms[i + a, 48:64, :].reshape(2, ROWS, lanes)
            parts += [main * own, main * shift, side * edge]
        high, low = split(jnp.concatenate(parts, axis=0).reshape(224, lanes))
        return dot16(m_hi[...], high) + dot16(m_hi[...], low) + dot16(m_lo[...], high)

    def element_pass(field, rows, take, init):
        prepare(0, field, rows)
        prepare(1, field, rows)
        before[...] = layer_forces(0)[48:96]

        def step(i, carry):
            prepare(i + 1, field, rows)
            out = layer_forces(i)
            total = out[0:48] + before[...]
            before[...] = out[48:96]
            return take(i, total[0:24] + behind(total[24:48]), carry)

        return lax.fori_loop(1, nx + 1, step, init)

    def fold(value):
        return value[0:8] + value[8:16] + value[16:24]

    wait_halo(0, u_f, u_h)

    def take_start(i, force, carry):
        residual = (loads[i - 1] - force) * over_cases(free[i - 1])
        d_f[i] = residual
        return carry + fold(residual * residual)

    norm_part = element_pass(u_f, u_h, take_start, no_rows)
    send_halo(1, d_f, d_h)
    wait_halo(1, d_f, d_h)

    def take_first(i, force, carry):
        image = force * over_cases(free[i - 1])
        q_f[i] = image
        return carry + fold(image * d_f[i])

    inner_part = element_pass(d_f, d_h, take_first, no_rows)
    send_sums(0, (inner_part, norm_part))
    send_halo(2, q_f, q_h)
    total = wait_sums(0)
    norm_now = total[count : 2 * count]
    step_length = widen(norm_now / total[0:count])
    norm_part = no_rows
    for x in range(1, nx + 1):
        residual = d_f[x] - step_length * q_f[x]
        r_f[x] = residual
        norm_part = norm_part + fold(residual * residual)
    send_sums(1, (norm_part,))
    wait_halo(2, q_f, q_h)
    for x in (0, nx + 1):
        r_f[x] = d_f[x] - step_length * q_f[x]
    for x in range(nx + 2):
        r_h[x] = d_h[x] - step_length * q_h[x]
        u_f[x] = u_f[x] + step_length * d_f[x]
        u_h[x] = u_h[x] + step_length * d_h[x]

    def take_second(i, force, carry):
        g_f[i - 1] = force * over_cases(free[i - 1])
        return carry

    element_pass(r_f, r_h, take_second, 0)
    norm_next = wait_sums(1)[0:count]
    ratio = widen(norm_next / norm_now)
    inner_part = no_rows
    for x in range(1, nx + 1):
        direction = r_f[x] + ratio * d_f[x]
        r_f[x] = direction
        inner_part = inner_part + fold(direction * (g_f[x - 1] + ratio * q_f[x]))
    send_sums(2, (inner_part,))
    for x in (0, nx + 1):
        r_f[x] = r_f[x] + ratio * d_f[x]
    for x in range(nx + 2):
        r_h[x] = r_h[x] + ratio * d_h[x]
    step_length = widen(norm_next / wait_sums(2)[0:count])
    for x in range(nx + 2):
        moved = u_f[x] + step_length * r_f[x]
        u_f[x] = moved
        u_h[x] = u_h[x] + step_length * r_h[x]
        if 1 <= x <= nx:
            for c in range(count):
                for comp in range(3):
                    disp_ref[c, comp, x - 1] = moved[
                        8 * comp : 8 * comp + 8, c * LANES : (c + 1) * LANES
                    ]

    weights = [weights_ref[case * count + c].astype(jnp.float32) for c in range(count)]
    wide_rows = lax.broadcasted_iota(jnp.int32, (ROWS, lanes), 0)

    def raised(p):
        edge_on = jnp.where(sub == 0, 1.0, 0.0)
        blocks = []
        for c in (0, 1):
            edge = terms[p, 48 + 8 * c : 56 + 8 * c, :] * edge_on
            for comp in range(3):
                start = 24 * c + 8 * comp
                block = pltpu.roll(terms[p, start : start + 8, :], 7, 0)
                blocks.append(jnp.where(wide_rows == 7, edge[comp : comp + 1], block))
        return jnp.concatenate(blocks, axis=0)

    prepare(1, u_f, u_h)

    def energy_step(i, carry):
        prepare(i + 1, u_f, u_h)
        both = terms[pl.ds(i, 2)].reshape(128, lanes)
        high, low = split(both)
        out = dot16(n_hi[...], high) + dot16(n_hi[...], low) + dot16(n_lo[...], high)
        found = no_rows
        for a in (0, 1):
            for b in (0, 1):
                value = raised(i + a) if b else terms[i + a, 0:48, :]
                base = 96 * a + 48 * b
                product = (value * out[base : base + 48]).reshape(6, ROWS, lanes)
                found = found + jnp.sum(product, axis=0)
        weighted = no_tile
        for c in range(count):
            weighted = weighted + weights[c] * found[:, c * LANES : (c + 1) * LANES]
        energy[i - 1] = weighted
        return carry

    lax.fori_loop(1, nx + 1, energy_step, 0)

    copies = [
        remote(energy, energy_in.at[n - 1], esend_sem.at[n - 1], erecv_sem.at[n - 1], case_peer(n))
        for n in range(1, cases)
    ]
    for copy in copies:
        copy.start()
    for copy in copies:
        copy.wait()
    weight_sum = weights_ref[0].astype(jnp.float32)
    for n in range(1, weights_ref.shape[0]):
        weight_sum = weight_sum + weights_ref[n].astype(jnp.float32)
    share = LANES // cases
    for x in range(nx):
        total = energy[x]
        for n in range(cases - 1):
            total = total + energy_in[n, x]
        density = dens_ref[x]
        result = -(PENALTY * (1.0 - SOFT_FLOOR)) * (density * density) * total / weight_sum
        owned = result[:, 0:share]
        for n in range(1, cases):
            owned = jnp.where(case == n, result[:, n * share : (n + 1) * share], owned)
        sens_ref[x] = owned


def per_device(
    mesh_shape, densities, fixed_mask, start_field, load_nodes, load_forces, case_weights, stiffness
):
    bricks, cases = mesh_shape["brick"], mesh_shape["case"]
    assert mesh_shape["sub"] == 2
    count, _, nx, ny, nz = start_field.shape
    assert ny == ROWS and nz == LANES
    lanes = count * LANES
    group = 2 * bricks
    sum_rows = -(-2 * count // 8) * 8
    pick, spread, keep = force_constants()
    pick3, spread3, keep3 = energy_constants()
    f32, bf16 = jnp.float32, jnp.bfloat16
    vmem = pl.BlockSpec(memory_space=pltpu.VMEM)
    smem = pl.BlockSpec(memory_space=pltpu.SMEM)
    dma = pltpu.SemaphoreType.DMA
    plane = pltpu.VMEM((nx + 2, 24, lanes), f32)
    rows = pltpu.VMEM((nx + 2, ROWS, lanes), f32)
    scales = pltpu.VMEM((nx + 1, ROWS, LANES), f32)
    return pl.pallas_call(
        functools.partial(kernel, (bricks, cases, count, nx, 2 * ROWS)),
        out_shape=(
            jax.ShapeDtypeStruct(start_field.shape, f32),
            jax.ShapeDtypeStruct((nx, ROWS, LANES // cases), f32),
        ),
        in_specs=[vmem] * 5 + [smem] + [vmem] * 7,
        out_specs=(vmem, vmem),
        scratch_shapes=[
            plane, plane, plane, plane,
            pltpu.VMEM((nx, 24, lanes), f32),
            rows, rows, rows, rows,
            pltpu.VMEM((3, nx, ROWS, lanes), f32),
            pltpu.VMEM((nx + 2, 64, lanes), f32),
            pltpu.VMEM((48, lanes), f32),
            pltpu.VMEM((nx, 24, lanes), f32),
            pltpu.VMEM((nx, 24, LANES), f32),
            scales, scales, scales, scales, scales,
            pltpu.VMEM((96, 224), bf16),
            pltpu.VMEM((96, 224), bf16),
            pltpu.VMEM((192, 128), bf16),
            pltpu.VMEM((192, 128), bf16),
            pltpu.VMEM((3, group - 1, sum_rows, LANES), f32),
            pltpu.VMEM((3, sum_rows, LANES), f32),
            pltpu.VMEM((nx, ROWS, LANES), f32),
            pltpu.VMEM((max(cases - 1, 1), nx, ROWS, LANES), f32),
            dma((3, 5)), dma((3, 5)), dma((3,)), dma((3,)),
            dma((3, group - 1)), dma((3, group - 1)),
            dma((max(cases - 1, 1),)), dma((max(cases - 1, 1),)),
        ],
        compiler_params=pltpu.CompilerParams(
            collective_id=0, has_side_effects=True, vmem_limit_bytes=40 * 2**20
        ),
    )(
        densities, fixed_mask, start_field, load_nodes, jnp.swapaxes(load_forces, 1, 2),
        case_weights, stiffness, *(jnp.asarray(x) for x in (pick, spread, keep, pick3, spread3, keep3)),
    )


def solution(mesh):
    return jax.shard_map(
        functools.partial(per_device, dict(mesh.shape)),
        mesh=mesh,
        in_specs=(
            P(("design", "brick"), "sub", None),
            P(None, ("design", "brick"), "sub", None),
            P("case", None, ("design", "brick"), "sub", None),
            P("case", None),
            P("case", None, None),
            P(),
            P(),
        ),
        out_specs=(
            P("case", None, ("design", "brick"), "sub", None),
            P(("design", "brick"), "sub", "case"),
        ),
        check_vma=False,
    )
```

time: 339 us -> 50 us (0.15); the launches traced: 335 us -> 49.4 us
  matrix products: 156 us -> 0 us
  blocking collectives: 49.8 us -> 0 us
  other arithmetic: 49.7 us -> 0 us
  Pallas kernels: 0 us -> 38.1 us
  starting transfers between devices: 33.4 us -> 0 us
  waiting for transfers between devices: 19.4 us -> 0 us
  local copies, waits for them, and re-layouts: 24.6 us -> 10.7 us
    dot_general x32 -> x0, matrix products: 156 us -> none  [element_terms(): jnp.einsum('ij,cjxyz->cixyz', stiffness[:, 3 * k:3 * k + 3], views[k], pr...]
    psum x4 -> x0, blocking collectives: 49.8 us -> none  [the longest x2 27.3 us: square_sums(): lax.psum(jnp.sum(residual * residual, axis=(1, 2, 3, 4)), ('brick', 'sub'))]
    pallas_call x0 -> x1, Pallas kernels: none -> 38.1 us  [per_device(): pl.pallas_call(functools.partial(kernel, (bricks, cases, count, nx, 2 * R...]
    ppermute x18 -> x0, starting transfers between devices: 33.4 us -> none  [the longest x8 16.2 us: padded_2(): lax.ppermute(tail, axis, [(i, (i + 1) % count) for i in range(ends)])]
    scatter-add x2 -> x0, other arithmetic: 31.8 us -> none  [place_loads(): return blank.at[:, targets].add(forces.T.astype(jnp.float32), mode='drop')]
    ppermute x18 -> x0, waiting for transfers between devices: 19.4 us -> none  [the longest x8 17.8 us: padded_2(): lax.ppermute(head, axis, [((i + 1) % count, i) for i in range(ends)])]
    reshape x1 -> x0, local copies, waits for them, and re-layouts: 10.7 us -> none  [per_device(): right_side.reshape(case_count, 3, cells_x, cells_y, cells_z) * free_mask]
    unnamed x9 -> x27, local copies, waits for them, and re-layouts: 0.81 us -> 10.7 us
  transfers between devices with their start and end apart: 18 -> 0, of which waited for: 10 -> 0; matrix products, arithmetic and copies ran while one was open for 16% -> 0% of each run, Pallas kernels for 0% -> 0%
where the time goes in v1:
time: 50 us; the launch traced here: 49.4 us
  Pallas kernels  38.1 us (76%)
  local copies, waits for them, and re-layouts  10.7 us (21%)
  between operations  0.67 us (1%)
    pallas_call x1, Pallas kernels, per_device(): pl.pallas_call(functools.partial(kernel, (bricks, cases, count, nx, 2 * R...  38.1 us
    unnamed x27, local copies, waits for them, and re-layouts  10.7 us

profile of v1, /device:TPU:0, one launch (start us, length us, event | category | flops | bytes accessed | tf_op | source)
XLA Modules:
  0.0 49.4 jit_solution(3014671363171123365)
XLA Ops:
  0.6 0.0 copy-start.9
  0.6 0.0 copy-start.10
  0.7 0.7 %copy.17 = s32[4,64,3]{1,2,0:T(4,128)S(1)} copy(s32[4,64,3]{1,0,2:T(4,128)} %param.17) | data formatting | bytes 6144 | tf_op args[4]
  1.4 0.0 copy-start.11
  1.4 0.0 copy-done.9
  1.4 0.0 copy-done.10
  1.4 0.6 %copy-done.11 = s32[8]{0:T(128)S(1)} copy-done((s32[8]{0:T(128)S(1)}, s32[8]{0:T(128)}, u32[]{:S(2)}) %copy-start.11) | copy-done | bytes 56
  2.0 0.0 copy-start
  2.0 1.0 %copy-done = f32[4,3,8,8,128]{4,3,2,1,0:T(8,128)S(1)} copy-done((f32[4,3,8,8,128]{4,3,2,1,0:T(8,128)S(1)}, f32[4,3,8,8,128]{4,3,2,1,0:T(8,128)}, u32[]{:S(2)}) %copy-start) | copy-done | bytes 393240
  3.0 0.0 copy-start.1
  3.0 1.0 %copy-done.1 = f32[2,2,192,128]{3,2,1,0:T(8,128)S(1)} copy-done((f32[2,2,192,128]{3,2,1,0:T(8,128)S(1)}, f32[2,2,192,128]{3,2,1,0:T(8,128)}, u32[]{:S(2)}) %copy-start.1) | copy-done | bytes 393240
  4.0 0.0 copy-start.2
  4.0 1.0 %copy-done.2 = f32[2,2,96,224]{3,2,1,0:T(8,128)S(1)} copy-done((f32[2,2,96,224]{3,2,1,0:T(8,128)S(1)}, f32[2,2,96,224]{3,2,1,0:T(8,128)}, u32[]{:S(2)}) %copy-start.2) | copy-done | bytes 344088
  5.0 0.0 copy-start.3
  5.0 0.9 %copy-done.3 = s32[3,8,8,128]{3,2,1,0:T(8,128)S(1)} copy-done((s32[3,8,8,128]{3,2,1,0:T(8,128)S(1)}, s32[3,8,8,128]{3,2,1,0:T(8,128)}, u32[]{:S(2)}) %copy-start.3) | copy-done | bytes 98328
  5.9 0.0 copy-start.4
  5.9 0.9 %copy-done.4 = f32[192,24]{1,0:T(8,128)S(1)} copy-done((f32[192,24]{1,0:T(8,128)S(1)}, f32[192,24]{1,0:T(8,128)}, u32[]{:S(2)}) %copy-start.4) | copy-done | bytes 18456
  6.8 0.0 copy-start.5
  6.8 0.9 %copy-done.5 = f32[2,96,24]{2,1,0:T(8,128)S(1)} copy-done((f32[2,96,24]{2,1,0:T(8,128)S(1)}, f32[2,96,24]{2,1,0:T(8,128)}, u32[]{:S(2)}) %copy-start.5) | copy-done | bytes 18456
  7.7 0.0 copy-start.6
  7.7 0.8 %copy-done.6 = f32[2,24,224]{2,1,0:T(8,128)S(1)} copy-done((f32[2,24,224]{2,1,0:T(8,128)S(1)}, f32[2,24,224]{2,1,0:T(8,128)}, u32[]{:S(2)}) %copy-start.6) | copy-done | bytes 43032
  8.5 0.0 copy-start.7
  8.5 0.8 %copy-done.7 = f32[8,8,128]{2,1,0:T(8,128)S(1)} copy-done((f32[8,8,128]{2,1,0:T(8,128)S(1)}, f32[8,8,128]{2,1,0:T(8,128)}, u32[]{:S(2)}) %copy-start.7) | copy-done | bytes 32792
  9.2 0.0 copy-start.8
  9.2 0.7 %copy-done.8 = f32[2,24,128]{2,1,0:T(8,128)S(1)} copy-done((f32[2,24,128]{2,1,0:T(8,128)S(1)}, f32[2,24,128]{2,1,0:T(8,128)}, u32[]{:S(2)}) %copy-start.8) | copy-done | bytes 24600
  10.0 38.1 %shard_map.140 = (f32[4,3,8,8,128]{4,3,2,1,0:T(8,128)S(1)}, f32[8,8,64]{2,1,0:T(8,128)S(1)}) custom-call(f32[8,8,128]{2,1,0:T(8,128)S(1)} %copy-done.7, s32[3,8,8,128]{3,2,1,0:T(8,128)S(1)} %copy-done.3, f32[4,3,8,8,128]{4,3,2,1,0:T(8,128)S(1)} %copy-done, s32[4,64]{1,0:T(4,128)S(1)} %copy-done.10, s32[4,3,64]{2,1,0:T(4,128)S(1)} %bitcast.3, ...), custom_call_target="tpu_custom_call" | custom-call | tf_op jit(solution)/shard_map/pallas_call | solution.py:524
  48.1 0.7 %copy.20 = f32[4,3,8,8,128]{4,3,2,1,0:T(8,128)} copy(f32[4,3,8,8,128]{4,3,2,1,0:T(8,128)S(1)} %get-tuple-element.4) | data formatting | bytes 786432
  48.8 0.6 %copy.21 = f32[8,8,64]{2,1,0:T(8,128)} copy(f32[8,8,64]{2,1,0:T(8,128)S(1)} %get-tuple-element.5) | data formatting | bytes 32768
Async XLA Ops:
  0.6 0.7 %copy-start.9 = (f32[24,24]{1,0:T(8,128)S(1)}, f32[24,24]{1,0:T(8,128)}, u32[]{:S(2)}) copy-start(f32[24,24]{1,0:T(8,128)} %stiff_ref.1) | copy-start | bytes 6916
  0.6 0.7 %copy-start.10 = (s32[4,64]{1,0:T(4,128)S(1)}, s32[4,64]{1,0:T(4,128)}, u32[]{:S(2)}) copy-start(s32[4,64]{1,0:T(4,128)} %nodes_ref.1) | copy-start | bytes 3076
  1.4 0.7 %copy-start.11 = (s32[8]{0:T(128)S(1)}, s32[8]{0:T(128)}, u32[]{:S(2)}) copy-start(s32[8]{0:T(128)} %weights_ref.1) | copy-start | bytes 100
  2.0 1.0 %copy-start = (f32[4,3,8,8,128]{4,3,2,1,0:T(8,128)S(1)}, f32[4,3,8,8,128]{4,3,2,1,0:T(8,128)}, u32[]{:S(2)}) copy-start(f32[4,3,8,8,128]{4,3,2,1,0:T(8,128)} %start_ref.1) | copy-start | bytes 1179652
  3.0 1.0 %copy-start.1 = (f32[2,2,192,128]{3,2,1,0:T(8,128)S(1)}, f32[2,2,192,128]{3,2,1,0:T(8,128)}, u32[]{:S(2)}) copy-start(f32[2,2,192,128]{3,2,1,0:T(8,128)} %constant.17.clone.keep3_ref) | copy-start | bytes 1179652
  4.0 1.0 %copy-start.2 = (f32[2,2,96,224]{3,2,1,0:T(8,128)S(1)}, f32[2,2,96,224]{3,2,1,0:T(8,128)}, u32[]{:S(2)}) copy-start(f32[2,2,96,224]{3,2,1,0:T(8,128)} %constant.14.clone.keep_ref) | copy-start | bytes 1032196
  5.0 0.9 %copy-start.3 = (s32[3,8,8,128]{3,2,1,0:T(8,128)S(1)}, s32[3,8,8,128]{3,2,1,0:T(8,128)}, u32[]{:S(2)}) copy-start(s32[3,8,8,128]{3,2,1,0:T(8,128)} %mask_ref.1) | copy-start | bytes 294916
  5.9 0.9 %copy-start.4 = (f32[192,24]{1,0:T(8,128)S(1)}, f32[192,24]{1,0:T(8,128)}, u32[]{:S(2)}) copy-start(f32[192,24]{1,0:T(8,128)} %constant.15.clone.pick3_ref) | copy-start | bytes 55300
  6.8 0.9 %copy-start.5 = (f32[2,96,24]{2,1,0:T(8,128)S(1)}, f32[2,96,24]{2,1,0:T(8,128)}, u32[]{:S(2)}) copy-start(f32[2,96,24]{2,1,0:T(8,128)} %constant.12.clone.pick_ref) | copy-start | bytes 55300
  7.7 0.8 %copy-start.6 = (f32[2,24,224]{2,1,0:T(8,128)S(1)}, f32[2,24,224]{2,1,0:T(8,128)}, u32[]{:S(2)}) copy-start(f32[2,24,224]{2,1,0:T(8,128)} %constant.13.clone.spread_ref) | copy-start | bytes 129028
  8.5 0.8 %copy-start.7 = (f32[8,8,128]{2,1,0:T(8,128)S(1)}, f32[8,8,128]{2,1,0:T(8,128)}, u32[]{:S(2)}) copy-start(f32[8,8,128]{2,1,0:T(8,128)} %dens_ref.1) | copy-start | bytes 98308
  9.2 0.7 %copy-start.8 = (f32[2,24,128]{2,1,0:T(8,128)S(1)}, f32[2,24,128]{2,1,0:T(8,128)}, u32[]{:S(2)}) copy-start(f32[2,24,128]{2,1,0:T(8,128)} %constant.16.clone.spread3_ref) | copy-start | bytes 73732

commit v2 on v1

--- a/solution.py
+++ b/solution.py
@@ -11,6 +11,9 @@
 PENALTY = 3.0
 SOFT_FLOOR = 0.001
 MESH = pl.DeviceIdType.MESH
+UNROLL = 6
+ENERGY_UNROLL = 8
+VMEM_BYTES = 63 * 2**20 + 2**19
 ROWS = 8
 LANES = 128
 
@@ -94,9 +97,11 @@
 
 def kernel(
     sizes,
+    dens_hbm, mask_hbm, start_hbm, nodes_hbm, forces_hbm, weights_hbm, stiff_hbm,
+    pick_hbm, spread_hbm, keep_hbm, pick3_hbm, spread3_hbm, keep3_hbm,
+    disp_ref, sens_ref,
     dens_ref, mask_ref, start_ref, nodes_ref, forces_ref, weights_ref, stiff_ref,
-    pick_ref, spread_ref, keep_ref, pick3_ref, spread3_ref, keep3_ref,
-    disp_ref, sens_ref,
+    pick_ref, spread_ref, keep_ref, pick3_ref, spread3_ref, keep3_ref, load_sem, first,
     u_f, d_f, q_f, r_f, g_f, u_h, d_h, q_h, r_h, stage,
     terms, before, loads, free, dens_own, dens_side, s_own, s_shift, s_edge,
     m_hi, m_lo, n_hi, n_lo, sums, sums_out, energy, energy_in,
@@ -119,6 +124,19 @@
     def case_peer(k):
         return {"case": lax.rem(case + k, cases)}
 
+    inputs = (
+        (start_hbm, start_ref), (mask_hbm, mask_ref), (dens_hbm, dens_ref),
+        (stiff_hbm, stiff_ref), (spread_hbm.at[sub], spread_ref), (pick_hbm, pick_ref),
+        (keep_hbm.at[sub], keep_ref), (spread3_hbm, spread3_ref), (pick3_hbm, pick3_ref),
+        (keep3_hbm.at[sub], keep3_ref), (nodes_hbm, nodes_ref), (forces_hbm, forces_ref),
+        (weights_hbm, weights_ref),
+    )
+    fetches = [
+        pltpu.make_async_copy(src, dst, load_sem.at[n]) for n, (src, dst) in enumerate(inputs)
+    ]
+    for fetch in fetches:
+        fetch.start()
+
     barrier = pltpu.get_barrier_semaphore()
     for k in range(1, group):
         pl.semaphore_signal(barrier, inc=1, device_id=peer(k), device_id_type=MESH)
@@ -167,9 +185,11 @@
             copies[3].start()
             copies[4].start()
 
-    def wait_halo(k, field, rows):
+    def wait_side(k, field, rows):
+        halo_copies(k, field, rows)[0].wait()
+
+    def wait_ends(k, field, rows):
         copies = halo_copies(k, field, rows)
-        copies[0].wait()
 
         @pl.when(brick > 0)
         def _():
@@ -223,6 +243,9 @@
 
     def over_cases(tile):
         return jnp.concatenate([tile] * count, axis=1)
+
+    fetches[0].wait()
+    fetches[1].wait()
 
     for x in range(nx):
         for comp in range(3):
@@ -254,6 +277,7 @@
 
     pl.semaphore_wait(barrier, group - 1 + cases - 1)
     send_halo(0, u_f, u_h)
+    fetches[2].wait()
     copies = density_copies()
     copies[0].start()
 
@@ -262,14 +286,16 @@
         copies[1].start()
         copies[2].start()
 
+    for fetch in fetches[3:]:
+        fetch.wait()
     stiff = stiff_ref[...]
-    spread_stiff = exact_dot(stiff, spread_ref[sub])
-    matrix = keep_ref[sub, 0] * exact_dot(pick_ref[0], spread_stiff)
-    matrix = matrix + keep_ref[sub, 1] * exact_dot(pick_ref[1], spread_stiff)
+    spread_stiff = exact_dot(stiff, spread_ref[...])
+    matrix = keep_ref[0] * exact_dot(pick_ref[0], spread_stiff)
+    matrix = matrix + keep_ref[1] * exact_dot(pick_ref[1], spread_stiff)
     m_hi[...], m_lo[...] = split(matrix)
     matrix = None
     for b in (0, 1):
-        part = keep3_ref[sub, b] * exact_dot(pick3_ref[...], exact_dot(stiff, spread3_ref[b]))
+        part = keep3_ref[b] * exact_dot(pick3_ref[...], exact_dot(stiff, spread3_ref[b]))
         matrix = part if matrix is None else matrix + part
     high, low = split(matrix)
     n_hi[...] = high
@@ -289,7 +315,7 @@
         depth = lax.broadcasted_iota(jnp.int32, (LANES, load_count), 0) == place_z
         depth = jnp.where(depth, 1.0, 0.0).astype(jnp.bfloat16)
         for comp in range(3):
-            force = forces_ref[c, comp : comp + 1, :].astype(jnp.float32)
+            force = forces_ref[comp, c : c + 1, :].astype(jnp.float32)
             weighted = jnp.where(hit, force, 0.0).astype(jnp.bfloat16)
             block = lax.dot_general(
                 weighted, depth, (((1,), (1,)), ((), ())), preferred_element_type=jnp.float32
@@ -297,22 +323,11 @@
             for x in range(nx):
                 loads[x, 8 * comp : 8 * comp + 8, c * LANES : (c + 1) * LANES] = block[8 * x : 8 * x + 8]
 
-    copies = density_copies()
-    copies[0].wait()
-
-    @pl.when(brick < last)
-    def _():
-        copies[1].wait_send()
-        copies[2].wait_send()
-
-    @pl.when(brick > 0)
-    def _():
-        copies[1].wait_recv()
-        copies[2].wait_recv()
-
+    density_copies()[0].wait()
     row_number = lax.broadcasted_iota(jnp.int32, (ROWS, LANES), 0)
     dens_own[1 : nx + 1] = dens_ref[...]
-    for i in range(nx + 1):
+
+    def layer_scale(i):
         def scale_of(density):
             scale = SOFT_FLOOR + (1.0 - SOFT_FLOOR) * (density * density * density)
             return jnp.where(brick > 0, scale, 0.0) if i == 0 else scale
@@ -324,6 +339,9 @@
         s_own[i] = own
         s_shift[i] = jnp.where(row_number == 0, below_edge, pltpu.roll(own, 1, 0))
         s_edge[i] = jnp.where(sub > 0, below_edge, own_edge)
+
+    for i in range(1, nx + 1):
+        layer_scale(i)
 
     def by_case(value, shift, edge):
         parts = []
@@ -360,40 +378,67 @@
         high, low = split(jnp.concatenate(parts, axis=0).reshape(224, lanes))
         return dot16(m_hi[...], high) + dot16(m_hi[...], low) + dot16(m_lo[...], high)
 
-    def element_pass(field, rows, take, init):
-        prepare(0, field, rows)
+    def element_pass(field, rows, ends, take, init):
         prepare(1, field, rows)
-        before[...] = layer_forces(0)[48:96]
+        prepare(2, field, rows)
+        out = layer_forces(1)
+        first[...] = out[0:48]
+        before[...] = out[48:96]
 
         def step(i, carry):
-            prepare(i + 1, field, rows)
             out = layer_forces(i)
             total = out[0:48] + before[...]
             before[...] = out[48:96]
             return take(i, total[0:24] + behind(total[24:48]), carry)
 
-        return lax.fori_loop(1, nx + 1, step, init)
+        def inner(i, carry):
+            prepare(i + 1, field, rows)
+            return step(i, carry)
+
+        carry = lax.fori_loop(2, nx, inner, init, unroll=UNROLL)
+        ends()
+        prepare(0, field, rows)
+        prepare(nx + 1, field, rows)
+        total = first[...] + layer_forces(0)[48:96]
+        carry = take(1, total[0:24] + behind(total[24:48]), carry)
+        return step(nx, carry)
 
     def fold(value):
         return value[0:8] + value[8:16] + value[16:24]
 
-    wait_halo(0, u_f, u_h)
+    wait_side(0, u_f, u_h)
+
+    def start_ends():
+        copies = density_copies()
+
+        @pl.when(brick < last)
+        def _():
+            copies[1].wait_send()
+            copies[2].wait_send()
+
+        @pl.when(brick > 0)
+        def _():
+            copies[1].wait_recv()
+            copies[2].wait_recv()
+
+        layer_scale(0)
+        wait_ends(0, u_f, u_h)
 
     def take_start(i, force, carry):
         residual = (loads[i - 1] - force) * over_cases(free[i - 1])
         d_f[i] = residual
         return carry + fold(residual * residual)
 
-    norm_part = element_pass(u_f, u_h, take_start, no_rows)
+    norm_part = element_pass(u_f, u_h, start_ends, take_start, no_rows)
     send_halo(1, d_f, d_h)
-    wait_halo(1, d_f, d_h)
+    wait_side(1, d_f, d_h)
 
     def take_first(i, force, carry):
         image = force * over_cases(free[i - 1])
         q_f[i] = image
         return carry + fold(image * d_f[i])
 
-    inner_part = element_pass(d_f, d_h, take_first, no_rows)
+    inner_part = element_pass(d_f, d_h, lambda: wait_ends(1, d_f, d_h), take_first, no_rows)
     send_sums(0, (inner_part, norm_part))
     send_halo(2, q_f, q_h)
     total = wait_sums(0)
@@ -405,19 +450,21 @@
         r_f[x] = residual
         norm_part = norm_part + fold(residual * residual)
     send_sums(1, (norm_part,))
-    wait_halo(2, q_f, q_h)
-    for x in (0, nx + 1):
-        r_f[x] = d_f[x] - step_length * q_f[x]
-    for x in range(nx + 2):
+    wait_side(2, q_f, q_h)
+    for x in range(1, nx + 1):
         r_h[x] = d_h[x] - step_length * q_h[x]
-        u_f[x] = u_f[x] + step_length * d_f[x]
-        u_h[x] = u_h[x] + step_length * d_h[x]
+
+    def second_ends():
+        wait_ends(2, q_f, q_h)
+        for x in (0, nx + 1):
+            r_f[x] = d_f[x] - step_length * q_f[x]
+            r_h[x] = d_h[x] - step_length * q_h[x]
 
     def take_second(i, force, carry):
         g_f[i - 1] = force * over_cases(free[i - 1])
         return carry
 
-    element_pass(r_f, r_h, take_second, 0)
+    element_pass(r_f, r_h, second_ends, take_second, 0)
     norm_next = wait_sums(1)[0:count]
     ratio = widen(norm_next / norm_now)
     inner_part = no_rows
@@ -426,16 +473,17 @@
         r_f[x] = direction
         inner_part = inner_part + fold(direction * (g_f[x - 1] + ratio * q_f[x]))
     send_sums(2, (inner_part,))
-    for x in (0, nx + 1):
-        r_f[x] = r_f[x] + ratio * d_f[x]
-    for x in range(nx + 2):
+    r_f[nx + 1] = r_f[nx + 1] + ratio * d_f[nx + 1]
+    for x in range(1, nx + 2):
+        u_f[x] = u_f[x] + step_length * d_f[x]
+        u_h[x] = u_h[x] + step_length * d_h[x]
         r_h[x] = r_h[x] + ratio * d_h[x]
     step_length = widen(norm_next / wait_sums(2)[0:count])
-    for x in range(nx + 2):
+    for x in range(1, nx + 2):
         moved = u_f[x] + step_length * r_f[x]
         u_f[x] = moved
         u_h[x] = u_h[x] + step_length * r_h[x]
-        if 1 <= x <= nx:
+        if x <= nx:
             for c in range(count):
                 for comp in range(3):
                     disp_ref[c, comp, x - 1] = moved[
@@ -476,7 +524,7 @@
         energy[i - 1] = weighted
         return carry
 
-    lax.fori_loop(1, nx + 1, energy_step, 0)
+    lax.fori_loop(1, nx + 1, energy_step, 0, unroll=ENERGY_UNROLL)
 
     copies = [
         remote(energy, energy_in.at[n - 1], esend_sem.at[n - 1], erecv_sem.at[n - 1], case_peer(n))
@@ -516,20 +564,31 @@
     pick3, spread3, keep3 = energy_constants()
     f32, bf16 = jnp.float32, jnp.bfloat16
     vmem = pl.BlockSpec(memory_space=pltpu.VMEM)
-    smem = pl.BlockSpec(memory_space=pltpu.SMEM)
     dma = pltpu.SemaphoreType.DMA
     plane = pltpu.VMEM((nx + 2, 24, lanes), f32)
     rows = pltpu.VMEM((nx + 2, ROWS, lanes), f32)
     scales = pltpu.VMEM((nx + 1, ROWS, LANES), f32)
+    arguments = (
+        densities, fixed_mask, start_field, load_nodes, jnp.transpose(load_forces, (2, 0, 1)),
+        case_weights, stiffness,
+    )
     return pl.pallas_call(
         functools.partial(kernel, (bricks, cases, count, nx, 2 * ROWS)),
         out_shape=(
             jax.ShapeDtypeStruct(start_field.shape, f32),
             jax.ShapeDtypeStruct((nx, ROWS, LANES // cases), f32),
         ),
-        in_specs=[vmem] * 5 + [smem] + [vmem] * 7,
+        in_specs=[pl.BlockSpec(memory_space=pltpu.HBM)] * 13,
         out_specs=(vmem, vmem),
         scratch_shapes=[
+            *(pltpu.VMEM(x.shape, x.dtype) for x in arguments[:5]),
+            pltpu.SMEM(case_weights.shape, case_weights.dtype),
+            pltpu.VMEM(stiffness.shape, f32),
+            pltpu.VMEM(pick.shape, f32), pltpu.VMEM(spread.shape[1:], f32),
+            pltpu.VMEM(keep.shape[1:], f32),
+            pltpu.VMEM(pick3.shape, f32), pltpu.VMEM(spread3.shape, f32),
+            pltpu.VMEM(keep3.shape[1:], f32),
+            dma((13,)), pltpu.VMEM((48, lanes), f32),
             plane, plane, plane, plane,
             pltpu.VMEM((nx, 24, lanes), f32),
             rows, rows, rows, rows,
@@ -552,12 +611,9 @@
             dma((max(cases - 1, 1),)), dma((max(cases - 1, 1),)),
         ],
         compiler_params=pltpu.CompilerParams(
-            collective_id=0, has_side_effects=True, vmem_limit_bytes=40 * 2**20
+            collective_id=0, has_side_effects=True, vmem_limit_bytes=VMEM_BYTES
         ),
-    )(
-        densities, fixed_mask, start_field, load_nodes, jnp.swapaxes(load_forces, 1, 2),
-        case_weights, stiffness, *(jnp.asarray(x) for x in (pick, spread, keep, pick3, spread3, keep3)),
-    )
+    )(*arguments, *(jnp.asarray(x) for x in (pick, spread, keep, pick3, spread3, keep3)))
 
 
 def solution(mesh):

time: 50 us -> 33.7 us (0.67)
  local copies, waits for them, and re-layouts: 10.7 us -> 2.39 us
  Pallas kernels: 38.1 us -> 30.5 us
    unnamed x27 -> x4, local copies, waits for them, and re-layouts: 10.7 us -> 2.39 us
    pallas_call x1, Pallas kernels: 38.1 us -> 30.5 us  [per_device(): pl.pallas_call(functools.partial(kernel, (bricks, cases, count, nx, 2 * R...]
where the time goes in v2:
time: 33.7 us; the launch traced here: 33.5 us
  Pallas kernels  30.5 us (91%)
  local copies, waits for them, and re-layouts  2.39 us (7%)
  between operations  0.65 us (2%)
    pallas_call x1, Pallas kernels, per_device(): pl.pallas_call(functools.partial(kernel, (bricks, cases, count, nx, 2 * R...  30.5 us
    unnamed x4, local copies, waits for them, and re-layouts  2.39 us

profile of v2, /device:TPU:0, one launch (start us, length us, event | category | flops | bytes accessed | tf_op | source)
XLA Modules:
  0.0 33.5 jit_solution(9166390618770226957)
XLA Ops:
  0.6 30.5 %shard_map.140 = (f32[4,3,8,8,128]{4,3,2,1,0:T(8,128)}, f32[8,8,64]{2,1,0:T(8,128)}) custom-call(f32[8,8,128]{2,1,0:T(8,128)} %dens_hbm.1, s32[3,8,8,128]{3,2,1,0:T(8,128)} %mask_hbm.1, f32[4,3,8,8,128]{4,3,2,1,0:T(8,128)} %start_hbm.1, s32[4,64]{1,0:T(4,128)} %nodes_hbm.1, s32[3,4,64]{2,1,0:T(4,128)} %bitcast.1, s32[8]{0:T(128)} %weights_hbm.1, ...), custom_call_target="tpu_custom_call" | custom-call | tf_op jit(solution)/shard_map/pallas_call | solution.py:575
  31.1 0.0 copy-start
  31.1 1.8 %copy.17 = f32[4,3,8,8,128]{4,3,2,1,0:T(8,128)} copy(f32[4,3,8,8,128]{4,3,2,1,0:T(8,128)} %get-tuple-element.4) | data formatting | bytes 786432
  32.9 0.0 copy-done
  32.9 0.6 %copy.18 = f32[8,8,64]{2,1,0:T(8,128)} copy(f32[8,8,64]{2,1,0:T(8,128)S(1)} %copy-done) | data formatting | bytes 32768
Async XLA Ops:
  31.1 1.8 %copy-start = (f32[8,8,64]{2,1,0:T(8,128)S(1)}, f32[8,8,64]{2,1,0:T(8,128)}, u32[]{:S(2)}) copy-start(f32[8,8,64]{2,1,0:T(8,128)} %get-tuple-element.5) | copy-start | bytes 49156

commit v3 on v2

--- a/solution.py
+++ b/solution.py
@@ -439,50 +439,48 @@
         return carry + fold(image * d_f[i])
 
     inner_part = element_pass(d_f, d_h, lambda: wait_ends(1, d_f, d_h), take_first, no_rows)
+    send_halo(2, q_f, q_h)
     send_sums(0, (inner_part, norm_part))
-    send_halo(2, q_f, q_h)
-    total = wait_sums(0)
-    norm_now = total[count : 2 * count]
-    step_length = widen(norm_now / total[0:count])
-    norm_part = no_rows
-    for x in range(1, nx + 1):
-        residual = d_f[x] - step_length * q_f[x]
-        r_f[x] = residual
-        norm_part = norm_part + fold(residual * residual)
-    send_sums(1, (norm_part,))
     wait_side(2, q_f, q_h)
-    for x in range(1, nx + 1):
-        r_h[x] = d_h[x] - step_length * q_h[x]
-
-    def second_ends():
-        wait_ends(2, q_f, q_h)
-        for x in (0, nx + 1):
-            r_f[x] = d_f[x] - step_length * q_f[x]
-            r_h[x] = d_h[x] - step_length * q_h[x]
 
     def take_second(i, force, carry):
         g_f[i - 1] = force * over_cases(free[i - 1])
         return carry
 
-    element_pass(r_f, r_h, second_ends, take_second, 0)
-    norm_next = wait_sums(1)[0:count]
-    ratio = widen(norm_next / norm_now)
+    element_pass(q_f, q_h, lambda: wait_ends(2, q_f, q_h), take_second, 0)
+    total = wait_sums(0)
+    norm_now = total[count : 2 * count]
+    inner_now = total[0:count]
+    step_length = widen(norm_now / inner_now)
+    norm_part = no_rows
     inner_part = no_rows
+    cross_part = no_rows
     for x in range(1, nx + 1):
-        direction = r_f[x] + ratio * d_f[x]
-        r_f[x] = direction
-        inner_part = inner_part + fold(direction * (g_f[x - 1] + ratio * q_f[x]))
-    send_sums(2, (inner_part,))
-    r_f[nx + 1] = r_f[nx + 1] + ratio * d_f[nx + 1]
+        direction = d_f[x]
+        image = q_f[x]
+        residual = direction - step_length * image
+        residual_image = image - step_length * g_f[x - 1]
+        r_f[x] = residual
+        norm_part = norm_part + fold(residual * residual)
+        inner_part = inner_part + fold(residual * residual_image)
+        cross_part = cross_part + fold(residual * image + direction * residual_image)
+    send_sums(1, (norm_part, inner_part, cross_part))
+    r_f[nx + 1] = d_f[nx + 1] - step_length * q_f[nx + 1]
     for x in range(1, nx + 2):
+        r_h[x] = d_h[x] - step_length * q_h[x]
         u_f[x] = u_f[x] + step_length * d_f[x]
         u_h[x] = u_h[x] + step_length * d_h[x]
-        r_h[x] = r_h[x] + ratio * d_h[x]
-    step_length = widen(norm_next / wait_sums(2)[0:count])
+    total = wait_sums(1)
+    norm_next = total[0:count]
+    ratio = norm_next / norm_now
+    inner = total[count : 2 * count] + ratio * total[2 * count : 3 * count]
+    inner = inner + ratio * ratio * inner_now
+    step_length = widen(norm_next / inner)
+    ratio = widen(ratio)
     for x in range(1, nx + 2):
-        moved = u_f[x] + step_length * r_f[x]
+        moved = u_f[x] + step_length * (r_f[x] + ratio * d_f[x])
         u_f[x] = moved
-        u_h[x] = u_h[x] + step_length * r_h[x]
+        u_h[x] = u_h[x] + step_length * (r_h[x] + ratio * d_h[x])
         if x <= nx:
             for c in range(count):
                 for comp in range(3):
@@ -559,7 +557,7 @@
     assert ny == ROWS and nz == LANES
     lanes = count * LANES
     group = 2 * bricks
-    sum_rows = -(-2 * count // 8) * 8
+    sum_rows = -(-3 * count // 8) * 8
     pick, spread, keep = force_constants()
     pick3, spread3, keep3 = energy_constants()
     f32, bf16 = jnp.float32, jnp.bfloat16

time: 33.7 us -> 32 us (0.950)
  Pallas kernels: 30.5 us -> 28.8 us
    pallas_call x1, Pallas kernels: 30.5 us -> 28.8 us  [per_device(): pl.pallas_call(functools.partial(kernel, (bricks, cases, count, nx, 2 * R...]
where the time goes in v3:
time: 32 us; the launch traced here: 31.9 us
  Pallas kernels  28.8 us (90%)
  local copies, waits for them, and re-layouts  2.39 us (7%)
  between operations  0.65 us (2%)
    pallas_call x1, Pallas kernels, per_device(): pl.pallas_call(functools.partial(kernel, (bricks, cases, count, nx, 2 * R...  28.8 us
    unnamed x4, local copies, waits for them, and re-layouts  2.39 us

profile of v3, /device:TPU:0, one launch (start us, length us, event | category | flops | bytes accessed | tf_op | source)
XLA Modules:
  0.0 31.9 jit_solution(9764885623747534347)
XLA Ops:
  0.6 28.8 %shard_map.140 = (f32[4,3,8,8,128]{4,3,2,1,0:T(8,128)}, f32[8,8,64]{2,1,0:T(8,128)}) custom-call(f32[8,8,128]{2,1,0:T(8,128)} %dens_hbm.1, s32[3,8,8,128]{3,2,1,0:T(8,128)} %mask_hbm.1, f32[4,3,8,8,128]{4,3,2,1,0:T(8,128)} %start_hbm.1, s32[4,64]{1,0:T(4,128)} %nodes_hbm.1, s32[3,4,64]{2,1,0:T(4,128)} %bitcast.1, s32[8]{0:T(128)} %weights_hbm.1, ...), custom_call_target="tpu_custom_call" | custom-call | tf_op jit(solution)/shard_map/pallas_call | solution.py:573
  29.5 0.0 copy-start
  29.5 1.8 %copy.17 = f32[4,3,8,8,128]{4,3,2,1,0:T(8,128)} copy(f32[4,3,8,8,128]{4,3,2,1,0:T(8,128)} %get-tuple-element.4) | data formatting | bytes 786432
  31.3 0.0 copy-done
  31.3 0.6 %copy.18 = f32[8,8,64]{2,1,0:T(8,128)} copy(f32[8,8,64]{2,1,0:T(8,128)S(1)} %copy-done) | data formatting | bytes 32768
Async XLA Ops:
  29.5 1.8 %copy-start = (f32[8,8,64]{2,1,0:T(8,128)S(1)}, f32[8,8,64]{2,1,0:T(8,128)}, u32[]{:S(2)}) copy-start(f32[8,8,64]{2,1,0:T(8,128)} %get-tuple-element.5) | copy-start | bytes 49156

commit v4 on v3

--- a/solution.py
+++ b/solution.py
@@ -99,9 +99,9 @@
     sizes,
     dens_hbm, mask_hbm, start_hbm, nodes_hbm, forces_hbm, weights_hbm, stiff_hbm,
     pick_hbm, spread_hbm, keep_hbm, pick3_hbm, spread3_hbm, keep3_hbm,
-    disp_ref, sens_ref,
+    disp_hbm, sens_ref,
     dens_ref, mask_ref, start_ref, nodes_ref, forces_ref, weights_ref, stiff_ref,
-    pick_ref, spread_ref, keep_ref, pick3_ref, spread3_ref, keep3_ref, load_sem, first,
+    pick_ref, spread_ref, keep_ref, pick3_ref, spread3_ref, keep3_ref, load_sem, first, disp_ref, out_sem,
     u_f, d_f, q_f, r_f, g_f, u_h, d_h, q_h, r_h, stage,
     terms, before, loads, free, dens_own, dens_side, s_own, s_shift, s_edge,
     m_hi, m_lo, n_hi, n_lo, sums, sums_out, energy, energy_in,
@@ -134,14 +134,14 @@
     fetches = [
         pltpu.make_async_copy(src, dst, load_sem.at[n]) for n, (src, dst) in enumerate(inputs)
     ]
-    for fetch in fetches:
-        fetch.start()
-
     barrier = pltpu.get_barrier_semaphore()
     for k in range(1, group):
         pl.semaphore_signal(barrier, inc=1, device_id=peer(k), device_id_type=MESH)
     for k in range(1, cases):
         pl.semaphore_signal(barrier, inc=1, device_id=case_peer(k), device_id_type=MESH)
+
+    for fetch in fetches:
+        fetch.start()
 
     def remote(src, dst, send, recv, device):
         return pltpu.make_async_remote_copy(
@@ -168,21 +168,27 @@
 
     def send_halo(k, field, rows):
         line = 7 * (1 - sub)
-        stage[k] = jnp.zeros((nx, ROWS, lanes), jnp.float32)
+        copies = halo_copies(k, field, rows)
+
+        @pl.when(brick > 0)
+        def _():
+            copies[1].start()
+
+        @pl.when(brick < last)
+        def _():
+            copies[3].start()
+
         for x in range(nx):
             for comp in range(3):
                 stage[k, x, comp : comp + 1, :] = field[x + 1, pl.ds(8 * comp + line, 1), :]
-        copies = halo_copies(k, field, rows)
         copies[0].start()
 
         @pl.when(brick > 0)
         def _():
-            copies[1].start()
             copies[2].start()
 
         @pl.when(brick < last)
         def _():
-            copies[3].start()
             copies[4].start()
 
     def wait_side(k, field, rows):
@@ -244,6 +250,7 @@
     def over_cases(tile):
         return jnp.concatenate([tile] * count, axis=1)
 
+    stage[...] = jnp.zeros(stage.shape, jnp.float32)
     fetches[0].wait()
     fetches[1].wait()
 
@@ -488,6 +495,9 @@
                         8 * comp : 8 * comp + 8, c * LANES : (c + 1) * LANES
                     ]
 
+    leave = pltpu.make_async_copy(disp_ref, disp_hbm, out_sem)
+    leave.start()
+
     weights = [weights_ref[case * count + c].astype(jnp.float32) for c in range(count)]
     wide_rows = lax.broadcasted_iota(jnp.int32, (ROWS, lanes), 0)
 
@@ -546,6 +556,7 @@
         for n in range(1, cases):
             owned = jnp.where(case == n, result[:, n * share : (n + 1) * share], owned)
         sens_ref[x] = owned
+    leave.wait()
 
 
 def per_device(
@@ -577,7 +588,7 @@
             jax.ShapeDtypeStruct((nx, ROWS, LANES // cases), f32),
         ),
         in_specs=[pl.BlockSpec(memory_space=pltpu.HBM)] * 13,
-        out_specs=(vmem, vmem),
+        out_specs=(pl.BlockSpec(memory_space=pltpu.HBM), vmem),
         scratch_shapes=[
             *(pltpu.VMEM(x.shape, x.dtype) for x in arguments[:5]),
             pltpu.SMEM(case_weights.shape, case_weights.dtype),
@@ -587,6 +598,7 @@
             pltpu.VMEM(pick3.shape, f32), pltpu.VMEM(spread3.shape, f32),
             pltpu.VMEM(keep3.shape[1:], f32),
             dma((13,)), pltpu.VMEM((48, lanes), f32),
+            pltpu.VMEM(start_field.shape, f32), dma(()),
             plane, plane, plane, plane,
             pltpu.VMEM((nx, 24, lanes), f32),
             rows, rows, rows, rows,

time: 32 us -> 32 us (level)
  no operation moved by 1% of the time
where the time goes in v4:
time: 32 us; the launch traced here: 31.8 us
  Pallas kernels  28.8 us (90%)
  local copies, waits for them, and re-layouts  2.39 us (7%)
  between operations  0.65 us (2%)
    pallas_call x1, Pallas kernels, per_device(): pl.pallas_call(functools.partial(kernel, (bricks, cases, count, nx, 2 * R...  28.8 us
    unnamed x4, local copies, waits for them, and re-layouts  2.39 us

profile of v4, /device:TPU:0, one launch (start us, length us, event | category | flops | bytes accessed | tf_op | source)
XLA Modules:
  0.0 31.8 jit_solution(8971862180618868913)
XLA Ops:
  0.6 28.8 %shard_map.140 = (f32[4,3,8,8,128]{4,3,2,1,0:T(8,128)}, f32[8,8,64]{2,1,0:T(8,128)}) custom-call(f32[8,8,128]{2,1,0:T(8,128)} %dens_hbm.1, s32[3,8,8,128]{3,2,1,0:T(8,128)} %mask_hbm.1, f32[4,3,8,8,128]{4,3,2,1,0:T(8,128)} %start_hbm.1, s32[4,64]{1,0:T(4,128)} %nodes_hbm.1, s32[3,4,64]{2,1,0:T(4,128)} %bitcast.1, s32[8]{0:T(128)} %weights_hbm.1, ...), custom_call_target="tpu_custom_call" | custom-call | tf_op jit(solution)/shard_map/pallas_call | solution.py:584
  29.4 0.0 copy-start
  29.4 1.8 %copy.17 = f32[4,3,8,8,128]{4,3,2,1,0:T(8,128)} copy(f32[4,3,8,8,128]{4,3,2,1,0:T(8,128)} %get-tuple-element.4) | data formatting | bytes 786432
  31.2 0.0 copy-done
  31.2 0.6 %copy.18 = f32[8,8,64]{2,1,0:T(8,128)} copy(f32[8,8,64]{2,1,0:T(8,128)S(1)} %copy-done) | data formatting | bytes 32768
Async XLA Ops:
  29.4 1.8 %copy-start = (f32[8,8,64]{2,1,0:T(8,128)S(1)}, f32[8,8,64]{2,1,0:T(8,128)}, u32[]{:S(2)}) copy-start(f32[8,8,64]{2,1,0:T(8,128)} %get-tuple-element.5) | copy-start | bytes 49156
